TPU v7x, 32 devices: a whole 2x2x4 slice. The times are simulated.
32 devices in a mesh: groups: 2 (over y), tm: 4 (over z), space: 2 (over x), chan: 2 (over core).
Axes of the slice: x: 2, y: 2, z: 4, core: 2. Of those that a mesh axis runs over, the one named last changes fastest.
Arguments:
- frames: bfloat16 [32, 64, 64, 256], P(('groups', 'tm'), 'chan', 'space'), parts along dimension 0, may hold values from -6 to 6
- conv_taps: float32 [64, 9], P('chan'), may hold values from -2 to 2
- pooling: float32 [64, 256], P('space'), may hold values from -0.0625 to 0.0625
- gain_matrix: float32 [256, 128], P(None, ('space', 'chan')), may hold values from -0.5 to 0.5
- transition: float32 [256, 256], replicated, as said below
- update_map: float32 [256, 256], replicated, as said below
- quiet_root: float32 [256, 256], replicated, as said below
- observed_root: float32 [256, 256], replicated, as said below
- init_mean: float32 [512], P('groups'), parts along dimension 0, may hold values from -6 to 6
- init_root: float32 [512, 256], P('groups'), parts along dimension 0, as said below
- observed: int32 [32], P(('groups', 'tm')), parts along dimension 0, may hold values 0 or 1
Outputs:
- filtered_means: float32 [32, 256], P(('groups', 'tm')), parts along dimension 0
- block_roots: float32 [8, 256, 256], P(('groups', 'tm')), parts along dimension 0
- tap_gradient: float32 [8, 64, 9], P(('groups', 'tm'), 'chan'), parts along dimension 0
There are 2 independent parts, one for each index of `groups`. A program takes and returns all parts, laid end to end along the dimension named above; an argument that names none is the same for every part. Nothing has to cross between parts.
Inputs may be any that keep to these rules, and one draw needn't show every extreme that they name: transition and update_map are upper triangular, with the same diagonal entries where these exceed 0.8. transition is upper triangular. `quiet_root`: upper triangular with a positive diagonal. `observed_root`: upper triangular with a positive diagonal. `init_root`: upper triangular with a positive diagonal.
All inputs are finite; a program needn't handle non-finite values. No bound on the sum of `observed` on one device may be relied on, other than what follows from the above.
Results may differ from a plain program's by a relative error of at most 0.0003.
Values may be sent and summed in bfloat16 or wider, within the bound.
A program may use at most 64 MiB of HBM per device.

v0:
```python
import jax
import jax.numpy as jnp
from jax import lax
from jax.sharding import PartitionSpec as P

DILATION_STEP = 2


precise = lax.Precision.HIGHEST


def extended(block, sides, width):
    for axis, dim in sides:
        count = lax.axis_size(axis)
        forward = [(i, i + 1) for i in range(count - 1)]
        backward = [(target, source) for source, target in forward]
        low = lax.ppermute(
            lax.slice_in_dim(block, block.shape[dim] - width, None, axis=dim), axis, forward
        )
        high = lax.ppermute(lax.slice_in_dim(block, 0, width, axis=dim), axis, backward)
        block = jnp.concatenate([low, block, high], axis=dim)
    return block


def prefix(value, axis, join, neutral):
    count, mine = (lax.axis_size(axis), lax.axis_index(axis))
    pieces = jax.tree.map(lambda part: lax.all_gather(part, axis), value)
    running = jax.tree.map(
        lambda part, zero: jnp.full_like(part, 0) + jnp.asarray(zero, part.dtype), value, neutral
    )

    def turn(position, running):
        longer = join(running, jax.tree.map(lambda part: part[position], pieces))
        return jax.tree.map(lambda new, old: jnp.where(position < mine, new, old), longer, running)

    return lax.fori_loop(0, count - 1, turn, running)


def gram_of(root_matrix):
    return jnp.dot(
        root_matrix.T, root_matrix, precision=precise, preferred_element_type=jnp.float32
    )


def merge_elements(earlier, later):
    first_map, first_shift, first_gram = earlier
    second_map, second_shift, second_gram = later
    joined_map = jnp.dot(
        second_map, first_map, precision=precise, preferred_element_type=jnp.float32
    )
    joined_shift = (
        jnp.dot(second_map, first_shift, precision=precise, preferred_element_type=jnp.float32)
        + second_shift
    )
    carried = jnp.dot(second_map, first_gram, precision=precise, preferred_element_type=jnp.float32)
    joined_gram = (
        jnp.dot(carried, second_map.T, precision=precise, preferred_element_type=jnp.float32)
        + second_gram
    )
    return (joined_map, joined_shift, joined_gram)


def local(
    frames,
    conv_taps,
    pooling,
    gain_matrix,
    transition,
    update_map,
    quiet_root,
    observed_root,
    init_mean,
    init_root,
    observed,
):
    step_count, channels, row_tiles, column_list = frames.shape
    width_state = transition.shape[0]
    extended_frame = extended(frames, (("space", 2),), DILATION_STEP)
    extended_frame = jnp.pad(
        extended_frame, ((0, 0), (0, 0), (0, 0), (DILATION_STEP, DILATION_STEP))
    ).astype(jnp.float32)
    window_views = [
        extended_frame[
            :,
            :,
            left_element * DILATION_STEP : left_element * DILATION_STEP + row_tiles,
            right_element * DILATION_STEP : right_element * DILATION_STEP + column_list,
        ]
        for left_element in range(3)
        for right_element in range(3)
    ]
    response = jnp.zeros(frames.shape, jnp.float32)
    for k in range(9):
        response = response + conv_taps[:, k][None, :, None, None] * window_views[k]
    weights = observed.astype(jnp.float32)
    tile_sums = jnp.einsum("tchw,hw->tc", response, pooling, precision=precise)
    gain_part = (
        jnp.dot(tile_sums, gain_matrix.T, precision=precise, preferred_element_type=jnp.float32)
        * weights[:, None]
    )
    shifts = lax.psum(gain_part, ("space", "chan"))
    scaling = weights / (row_tiles * lax.axis_size("space") * column_list)
    grad_local = jnp.stack(
        [
            jnp.sum(response * window_views[k] * scaling[:, None, None, None], axis=(0, 2, 3))
            for k in range(9)
        ],
        axis=1,
    )
    tap_gradient = lax.psum(grad_local, "space")[None]
    is_seen = observed > 0
    step_maps = jnp.where(is_seen[:, None, None], update_map[None], transition[None])
    observed_gram = gram_of(observed_root)
    quiet_gram = gram_of(quiet_root)
    step_grams = jnp.where(is_seen[:, None, None], observed_gram[None], quiet_gram[None])
    unit_matrix = jnp.eye(width_state, dtype=jnp.float32)
    block_map, block_shift, block_gram = (step_maps[0], shifts[0], step_grams[0])
    for j in range(1, step_count):
        block_map, block_shift, block_gram = merge_elements(
            (block_map, block_shift, block_gram), (step_maps[j], shifts[j], step_grams[j])
        )
    identity = (
        unit_matrix,
        jnp.zeros((width_state,), jnp.float32),
        jnp.zeros((width_state, width_state), jnp.float32),
    )
    before = prefix((block_map, block_shift, block_gram), "tm", merge_elements, identity)
    state = merge_elements((unit_matrix, init_mean, gram_of(init_root)), before)
    mean_now = state[1]
    mean_list = []
    for j in range(step_count):
        mean_now = (
            jnp.dot(step_maps[j], mean_now, precision=precise, preferred_element_type=jnp.float32)
            + shifts[j]
        )
        mean_list.append(mean_now)
    filtered_means = jnp.stack(mean_list, axis=0)
    final_state = merge_elements(state, (block_map, block_shift, block_gram))
    block_roots = jnp.linalg.cholesky(final_state[2]).T[None]
    return (filtered_means, block_roots, tap_gradient)


def solution(mesh):
    return jax.shard_map(
        local,
        mesh=mesh,
        in_specs=(
            P(("groups", "tm"), "chan", "space", None),
            P("chan", None),
            P("space", None),
            P(None, ("space", "chan")),
            P(),
            P(),
            P(),
            P(),
            P("groups"),
            P("groups", None),
            P(("groups", "tm")),
        ),
        out_specs=(
            P(("groups", "tm"), None),
            P(("groups", "tm"), None, None),
            P(("groups", "tm"), "chan", None),
        ),
        check_vma=False,
    )
```

profile of v0, /device:TPU:0, one launch (start us, length us, event | category | flops | bytes accessed | tf_op | source)
XLA Modules:
  0.0 149.7 jit_solution(7803377094408503304)
XLA Ops:
  10.0 1.7 %fusion.52 = f32[256,256]{0,1:T(8,128)S(1)} fusion(f32[256,256]{1,0:T(8,128)} %param.19), kind=kOutput, calls=%fused_computation.112 | convolution fusion | flops 201326592 | bytes 524288 | tf_op jit(solution)/shard_map/dot_general | solution.py:40
  17.0 1.4 fusion.49
  18.5 4.8 %collective-permute-start = (bf16[4,32,2,256]{3,2,1,0:T(2,128)(2,1)S(1)}, bf16[4,32,2,256]{3,2,1,0:T(2,128)(2,1)S(1)}, u32[]{:S(2)}, u32[]{:S(2)}) collective-permute-start(bf16[4,32,2,256]{3,2,1,0:T(2,128)(2,1)S(1)} %get-tuple-element.222), channel_id=1, source_target_pairs={{0,2},{1,3},{4,6},{5,7},{8,10},{9,11},{12,14},{13,15},{16,18},{17,... | collective-permute-start | bytes 393224 | tf_op jit(solution)/shard_map/ppermute | solution.py:17
  23.3 1.5 collective-permute-start.1
  28.7 1.4 collective-permute-done.1
  30.2 4.8 %fusion.27 = f32[4,32,36,260]{3,2,1,0:T(8,128)S(1)} fusion(bf16[4,32,2,256]{3,2,1,0:T(2,128)(2,1)S(1)} %collective-permute-done.1, bf16[4,32,32,256]{3,2,1,0:T(8,128)(2,1)} %param.13, bf16[4,32,2,256]{3,2,1,0:T(2,128)(2,1)S(1)} %collective-permute-done), kind=kLoop, calls=%fused_computation.44 | loop fusion | flops 14376960 | bytes 7151616 | tf_op jit(solution)/shard_map/convert_element_type | solution.py:81
  35.0 11.3 %multiply_reduce_fusion = (f32[32]{0:T(128)S(1)}, f32[32]{0:T(128)S(1)}, f32[32]{0:T(128)S(1)}, f32[32]{0:T(128)S(1)}, f32[32]{0:T(128)S(1)}, /*index=5*/f32[32]...) fusion(f32[4,32,36,260]{3,2,1,0:T(8,128)S(1)} %fusion.27, ...), kind=kLoop, calls=%fused_computation.32 | loop fusion | flops 46137056 | bytes 41945360 | tf_op jit(solution)/shard_map/reduce_sum | solution.py:105
  46.3 5.0 %psum.15 = f32[1,32,9]{1,2,0:T(8,128)S(1)} all-reduce(f32[1,32,9]{1,2,0:T(8,128)S(1)} %bitcast.197), channel_id=1, replica_groups=mesh['groups'=2,'tm'=4,'space'=2,'chan'=2] {'space'}, use_global_device_ids=true, to_apply=%region_16.17 | all-reduce | flops 288 | bytes 2304 | tf_op jit(solution)/shard_map/psum | solution.py:110
  51.9 12.1 %fusion.23 = f32[1,4,32,1]{2,0,3,1:T(1,128)S(1)} fusion(f32[4,32,32,256]{3,2,1,0:T(8,128)} %get-tuple-element.221, f32[32,256,1,1]{1,0,2,3:T(8,128)S(1)} %bitcast.196), kind=kOutput, calls=%fused_computation.30 | convolution fusion | flops 12582912 | bytes 4227584 | tf_op jit(solution)/shard_map/tchw,hw->tc/dot_general | solution.py:96
  64.2 6.1 %psum.14 = f32[4,256]{1,0:T(4,128)S(1)} all-reduce(f32[4,256]{1,0:T(4,128)S(1)} %convolution_multiply_fusion), channel_id=1, replica_groups=mesh['groups'=2,'tm'=4,'space'=2,'chan'=2] {'space','chan'}, use_global_device_ids=true, to_apply=%region_0.1 | all-reduce | flops 1024 | bytes 8192 | tf_op jit(solution)/shard_map/psum | solution.py:101
  71.0 11.2 %all-gather.3 = f32[4,1,256]{2,1,0:T(1,128)S(1)} all-gather(f32[1,1,256]{2,1,0:T(1,128)S(1)} %bitcast.222), channel_id=3, replica_groups=mesh['groups'=2,'tm'=4,'space'=2,'chan'=2] {'tm'}, dimensions={0}, use_global_device_ids=true | all-gather | bytes 5120 | tf_op jit(solution)/shard_map/all_gather | solution.py:27
  82.2 1.6 %copy.41 = f32[1024,256]{1,0:T(8,128)S(1)} copy(f32[1024,256]{0,1:T(8,128)} %all-gather.9.cloned.1.call-done) | data formatting | bytes 2097152
  83.8 16.7 %while.18 = (s32[]{:T(128)}, f32[256,256]{1,0:T(8,128)S(1)}, f32[256]{0:T(256)S(1)}, f32[256,256]{1,0:T(8,128)S(1)}, s32[]{:T(128)}, /*index=5*/f32[4,256,256]{2...) while((s32[]{:T(128)}, f32[256,256]{1,0:T(8,128)S(1)}, ...), condition=%wide.region_2.3_spmd.clone, body=%wide.region_1.2_spmd.clone.sunk | while | flops 605094912 | bytes 3945090 | solution.py:36
  83.8 1.4 fusion.113
  85.2 1.4 fusion.114
  88.0 1.3 convolution_select_fusion.2
  89.4 1.3 fusion.113
  90.7 1.4 fusion.114
  94.8 1.3 fusion.113
  96.2 1.4 fusion.114
  102.7 1.4 convolution_add_fusion.1
  104.2 11.7 %cholesky.49 = f32[128,128]{1,0:T(8,128)S(1)} custom-call(f32[128,128]{1,0:T(8,128)S(1)} %cholesky.115), custom_call_target="Cholesky" | custom-call | tf_op jit(solution)/shard_map/jit(cholesky)/cholesky | solution.py:139
  116.0 9.8 %custom-call.11 = f32[1,128,128]{1,2,0:T(8,128)S(1)} custom-call(f32[1,128,128]{2,1,0:T(8,128)S(1)} %get-tuple-element.227), custom_call_target="InvertDiagBlocksLowerTriangular" | custom-call | tf_op jit(solution)/shard_map/jit(cholesky)/cholesky | solution.py:139
  126.3 11.7 %cholesky.103 = f32[128,128]{1,0:T(8,128)S(1)} custom-call(f32[128,128]{1,0:T(8,128)S(1)} %convolution_subtract_fusion), custom_call_target="Cholesky" | custom-call | tf_op jit(solution)/shard_map/jit(cholesky)/cholesky | solution.py:139
  (97 shorter events, 26.3 us)
Async XLA Ops:
  7.2 2.3 %copy-start = (f32[256,256]{1,0:T(8,128)S(1)}, f32[256,256]{1,0:T(8,128)}, u32[]{:S(2)}) copy-start(f32[256,256]{1,0:T(8,128)} %param.20) | copy-start | bytes 786436
  7.2 75.0 %all-gather.9.cloned.1.call-start = ((), (), s32[]{:S(2)}) async-start(), calls=%async_computation.1 | async-start | bytes 1310720 | tf_op jit(solution)/shard_map/all_gather | solution.py:27
  13.2 14.1 %copy-start.4 = (f32[32,9]{0,1:T(8,128)S(1)}, f32[32,9]{0,1:T(8,128)}, u32[]{:S(2)}) copy-start(f32[32,9]{0,1:T(8,128)} %param.14) | copy-start | bytes 3460
  13.2 14.2 %copy-start.2 = (f32[256,256]{1,0:T(8,128)S(1)}, f32[256,256]{1,0:T(8,128)}, u32[]{:S(2)}) copy-start(f32[256,256]{1,0:T(8,128)} %param.22) | copy-start | bytes 786436
  13.8 14.9 %copy-start.7 = (s32[4]{0:T(128)S(1)}, s32[4]{0:T(128)}, u32[]{:S(2)}) copy-start(s32[4]{0:T(128)} %param.23) | copy-start | bytes 52
  17.0 66.8 %all-gather.7.cloned.1.call-start = ((), (), s32[]{:S(2)}) async-start(), calls=%async_computation | async-start | bytes 1310720 | tf_op jit(solution)/shard_map/all_gather | solution.py:27
  18.5 10.3 %collective-permute-start = (bf16[4,32,2,256]{3,2,1,0:T(2,128)(2,1)S(1)}, bf16[4,32,2,256]{3,2,1,0:T(2,128)(2,1)S(1)}, u32[]{:S(2)}, u32[]{:S(2)}) collective-permute-start(bf16[4,32,2,256]{3,2,1,0:T(2,128)(2,1)S(1)} %get-tuple-element.222), channel_id=1, source_target_pairs={{0,2},{1,3},{4,6},{5,7},{8,10},{9,11},{12,14},{13,15},{16,18},{17,... | collective-permute-start | bytes 393224 | tf_op jit(solution)/shard_map/ppermute | solution.py:17
  23.3 6.9 %collective-permute-start.1 = (bf16[4,32,2,256]{3,2,1,0:T(2,128)(2,1)S(1)}, bf16[4,32,2,256]{3,2,1,0:T(2,128)(2,1)S(1)}, u32[]{:S(2)}, u32[]{:S(2)}) collective-permute-start(bf16[4,32,2,256]{3,2,1,0:T(2,128)(2,1)S(1)} %get-tuple-element.223), channel_id=1, source_target_pairs={{2,0},{3,1},{6,4},{7,5},{10,8},{11,9},{14,12},{15,13},{18,16},{19,... | collective-permute-start | bytes 393224 | tf_op jit(solution)/shard_map/ppermute | solution.py:20
  35.0 16.9 %copy-start.3 = (f32[32,256]{1,0:T(8,128)S(1)}, f32[32,256]{1,0:T(8,128)}, u32[]{:S(2)}) copy-start(f32[32,256]{1,0:T(8,128)} %param.15) | copy-start | bytes 98308
  46.3 17.8 %copy-start.6 = (f32[256,32]{0,1:T(8,128)S(1)}, f32[256,32]{0,1:T(8,128)}, u32[]{:S(2)}) copy-start(f32[256,32]{0,1:T(8,128)} %param.16) | copy-start | bytes 98308
  83.8 18.5 %copy-start.1 = (f32[256,256]{1,0:T(8,128)S(1)}, f32[256,256]{1,0:T(8,128)}, u32[]{:S(2)}) copy-start(f32[256,256]{1,0:T(8,128)} %fusion.36) | copy-start | bytes 786436
  100.5 40.4 %copy-start.5 = (f32[256]{0:T(256)S(1)}, f32[256]{0:T(256)}, u32[]{:S(2)}) copy-start(f32[256]{0:T(256)} %param.21) | copy-start | bytes 3076
Sparse Core Ops, SparseCore 0:
  17.1 30.6 all-gather.8
  49.9 27.4 all-gather.6
where the time goes:
time: 151 us; the launch traced here: 150 us
  other arithmetic  51.8 us (34%)
  matrix products  44.4 us (29%)
  blocking collectives  22.3 us (15%)
  between operations  15.8 us (10%)
  local copies, waits for them, and re-layouts  7.1 us (5%)
  starting transfers between devices  6.4 us (4%)
    another operation x6, other arithmetic, local(): block_roots = jnp.linalg.cholesky(final_state[2]).T[None]  33.9 us
    dot_general x1, matrix products, local(): tile_sums = jnp.einsum('tchw,hw->tc', response, pooling, precision=precise)  12.1 us
    reduce_sum x1, other arithmetic, local(): jnp.sum(response * window_views[k] * scaling[:, None, None, None], axis=(...  11.3 us
    all_gather x1, blocking collectives, prefix(): pieces = jax.tree.map(lambda part: lax.all_gather(part, axis), value)  11.2 us
    dot_general x8, matrix products, merge_elements(): jnp.dot(carried, second_map.T, precision=precise, preferred_element_type=...  8.5 us
    dot_general x8, matrix products, merge_elements(): jnp.dot(second_map, first_gram, precision=precise, preferred_element_type...  7.54 us
    dot_general x6, matrix products, merge_elements(): jnp.dot(second_map, first_map, precision=precise, preferred_element_type=...  6.49 us
    psum x1, blocking collectives, local(): shifts = lax.psum(gain_part, ('space', 'chan'))  6.1 us
  transfers between devices with their start and end apart: 4, of which 1 were waited for; matrix products, arithmetic and copies ran while one was open for 24% of the time, Pallas kernels for 0%

commit v1 on v0

v1 whole, which is shorter than its diff:
```python
import functools

import jax
import jax.numpy as jnp
from jax import lax
from jax.experimental import pallas as pl
from jax.experimental.pallas import tpu as pltpu
from jax.sharding import PartitionSpec as P

DILATION_STEP = 2
NB = 16
F32 = jnp.float32
BF16 = jnp.bfloat16
VMEM = pl.BlockSpec(memory_space=pltpu.VMEM)
SMEM = pl.BlockSpec(memory_space=pltpu.SMEM)

NT_DIMS = (((1,), (1,)), ((), ()))
TN_DIMS = (((0,), (0,)), ((), ()))
PAIRS = (((0, 0), 0), ((1, 1), 1), ((-1, -1), 2), ((0, 1), 3), ((-1, 0), 3), ((-1, 1), 4))


def moments_kernel(rows, group, position, inside, limit, flags, taps, x_ref, pools, taps_wide, grad_ref, sums_ref):
    steps, width = x_ref.shape[0], x_ref.shape[3]
    first = pl.program_id(0) * group
    for c in range(group):
        weight = taps[first + c, 0] * pools[0]
        for k in range(1, 9):
            weight = weight + taps[first + c, k] * pools[k]
        for t in range(steps):
            part = x_ref[t, c].astype(F32) * weight
            sums_ref[0, t * group + c : t * group + c + 1, :] = jnp.sum(part, axis=0, keepdims=True)
    lane = lax.broadcasted_iota(jnp.int32, (group * rows, width), 1)
    left, left_low, left_high, plain, by_one, by_two = [], [], [], [], [], []
    for t in range(steps):
        x = x_ref[t].reshape(group * rows, width).astype(F32)
        scaled = x * flags[t].astype(F32)
        left.append(scaled.astype(BF16))
        left_low.append(jnp.where(lane >= DILATION_STEP, scaled, 0.0).astype(BF16))
        left_high.append(jnp.where(lane < width - DILATION_STEP, scaled, 0.0).astype(BF16))
        plain.append(x.astype(BF16))
        one = pltpu.roll(x, width - DILATION_STEP, 1)
        by_one.append(jnp.where(lane < width - DILATION_STEP, one, 0.0).astype(BF16))
        two = pltpu.roll(x, width - 2 * DILATION_STEP, 1)
        by_two.append(jnp.where(lane < width - 2 * DILATION_STEP, two, 0.0).astype(BF16))
    cat = lambda pieces: jnp.concatenate(pieces, axis=1)
    left, plain = cat(left), cat(plain)
    size = group * rows
    lane_f = lax.broadcasted_iota(jnp.int32, (rows, size), 1)
    row_e = lax.broadcasted_iota(jnp.int32, (rows, size), 0)
    col_e = lax.rem(lane_f, rows)
    owner = lax.div(lane_f, rows)
    row_h, col_h = position(row_e), position(col_e)
    grads = [jnp.zeros((1, size), F32) for _ in range(9)]
    pairs = ((left, plain), (cat(left_low), plain), (cat(left_high), plain), (left, cat(by_one)), (left, cat(by_two)))
    for kind, (lhs, rhs) in enumerate(pairs):
        gram = lax.dot_general(lhs, rhs, NT_DIMS, preferred_element_type=F32)
        folded = jnp.zeros((rows, size), F32)
        for c in range(group):
            folded = jnp.where(owner == c, gram[c * rows : (c + 1) * rows, :], folded)
        for a in range(-1, 2):
            for z in range(-1, 2):
                h = row_h - DILATION_STEP * a
                keep = (h >= 0) & (h < limit) & (row_h - col_h == DILATION_STEP * (a - z)) & inside(row_e, col_e)
                row = jnp.sum(jnp.where(keep, folded, 0.0), axis=0, keepdims=True)
                for (b, y), which in PAIRS:
                    if which != kind:
                        continue
                    k, q = 3 * (a + 1) + b + 1, 3 * (z + 1) + y + 1
                    grads[k] = grads[k] + row * taps_wide[q : q + 1, :]
                    if b != y:
                        grads[q] = grads[q] + row * taps_wide[k : k + 1, :]
    for k in range(9):
        grad_ref[0, k : k + 1, :] = grads[k]


def moments(x, pools, conv_taps, flags, position, inside, limit):
    steps, channels, rows, width = x.shape
    group = min(channels, 256 // rows)
    groups = channels // group
    size = group * rows
    taps_wide = jnp.repeat(conv_taps.T, rows, axis=1)
    grads, sums = pl.pallas_call(
        functools.partial(moments_kernel, rows, group, position, inside, limit),
        grid=(groups,),
        in_specs=[
            SMEM,
            SMEM,
            pl.BlockSpec((steps, group, rows, width), lambda g: (0, g, 0, 0)),
            pl.BlockSpec((9, rows, width), lambda g: (0, 0, 0)),
            pl.BlockSpec((9, size), lambda g: (0, g)),
        ],
        out_specs=[
            pl.BlockSpec((1, 9, size), lambda g: (g, 0, 0)),
            pl.BlockSpec((1, steps * group, width), lambda g: (g, 0, 0)),
        ],
        out_shape=[
            jax.ShapeDtypeStruct((groups, 9, size), F32),
            jax.ShapeDtypeStruct((groups, steps * group, width), F32),
        ],
        compiler_params=pltpu.CompilerParams(vmem_limit_bytes=48 * 2**20),
        cost_estimate=pl.CostEstimate(flops=2 * 5 * groups * size * size * steps * width, bytes_accessed=x.size * 2, transcendentals=0),
    )(flags, conv_taps, x, pools, taps_wide)
    grads = jnp.sum(grads.reshape(groups, 9, group, rows), axis=3)
    sums = jnp.sum(sums, axis=2).reshape(groups, steps, group)
    return jnp.transpose(grads, (0, 2, 1)).reshape(channels, 9), jnp.transpose(sums, (1, 0, 2)).reshape(steps, channels)


def split2(x):
    high = x.astype(BF16)
    return high, (x - high.astype(F32)).astype(BF16)


def split3(x):
    high = x.astype(BF16)
    rest = x - high.astype(F32)
    mid = rest.astype(BF16)
    return high, mid, (rest - mid.astype(F32)).astype(BF16)


def gram3(x):
    h, m, l = split3(x)
    lhs = jnp.concatenate([h, h, m, h, l, m], axis=0)
    rhs = jnp.concatenate([h, m, h, l, h, m], axis=0)
    return lax.dot_general(lhs, rhs, TN_DIMS, preferred_element_type=F32)


def covariance_kernel(flags, quiet_map, seen_map, quiet_root, seen_root, init_root, out_ref, maps, maps_t, grams, cov, panel, held):
    size = out_ref.shape[0]
    total = flags.shape[0] - 1
    for index, (map_ref, root_ref) in enumerate(((quiet_map, quiet_root), (seen_map, seen_root))):
        h, l = split2(map_ref[...])
        maps[index] = jnp.concatenate([h, h, l], axis=1)
        h, l = split2(map_ref[...].T)
        maps_t[index] = jnp.concatenate([h, h, l], axis=0)
        grams[index] = gram3(root_ref[...])
    cov[...] = gram3(init_root[...])

    def advance(t, carry):
        flag = jnp.where(flags[t] > 0, 1, 0)
        h, l = split2(cov[...])
        moved = jnp.dot(maps[flag], jnp.concatenate([h, l, h], axis=0), preferred_element_type=F32)
        h, l = split2(moved)
        cov[...] = jnp.dot(jnp.concatenate([h, l, h], axis=1), maps_t[flag], preferred_element_type=F32) + grams[flag]
        return carry

    lax.fori_loop(0, flags[total], advance, 0)

    lane = lax.broadcasted_iota(jnp.int32, (8, size), 1)
    held[...] = jnp.zeros_like(held)
    panel[...] = cov[0:NB, :]

    def block(b, carry):
        start = pl.multiple_of(b * NB, NB)
        before = held[...]
        rows = panel[...]
        corner = pltpu.roll(rows, lax.rem(size - start, size), 1)[:, 0:128]
        wide = [jnp.broadcast_to(corner[:, k : k + 1], (NB, 128)) for k in range(NB)]
        d = [[None] * NB for _ in range(NB)]
        for k in range(NB):
            for i in range(k + 1):
                d[i][k] = jnp.broadcast_to(wide[k][i : i + 1, :], (8, 128))
        lines = [jnp.broadcast_to(panel[i : i + 1, :], (8, size)) for i in range(NB)]
        for j in range(NB):
            r = lax.rsqrt(d[j][j])
            r = r * (1.5 - 0.5 * d[j][j] * r * r)
            u = {k: d[j][k] * r for k in range(j + 1, NB)}
            twice = jnp.concatenate([r] * (size // 128), axis=1)
            line = jnp.where(lane >= start + j, lines[j] * twice, 0.0)
            held[j : j + 1, :] = line[0:1, :]
            for i in range(j + 1, NB):
                lines[i] = lines[i] - jnp.concatenate([u[i]] * (size // 128), axis=1) * line
                for k in range(i, NB):
                    d[i][k] = d[i][k] - u[i] * u[k]
        cov[...] = cov[...] - gram3(before)
        done = held[...]
        out_ref[pl.ds(start, NB), :] = done
        after = lax.rem(start + NB, size)
        turned = pltpu.roll(done, lax.rem(size - after, size), 1)[:, 0:128]
        h, m, l = split3(done)
        p, q, s = split3(turned)
        lhs = jnp.concatenate([p, p, q, p, s, q], axis=0)
        rhs = jnp.concatenate([h, m, h, l, h, m], axis=0)
        change = lax.dot_general(lhs, rhs, TN_DIMS, preferred_element_type=F32)
        panel[...] = cov[pl.ds(pl.multiple_of(after, NB), NB), :] - change[0:NB, :]
        return carry

    lax.fori_loop(0, size // NB, block, 0)


def covariance(flags_and_count, transition, update_map, quiet_root, observed_root, init_root):
    size = transition.shape[0]
    return pl.pallas_call(
        covariance_kernel,
        in_specs=[SMEM] + [VMEM] * 5,
        out_specs=VMEM,
        out_shape=jax.ShapeDtypeStruct((size, size), F32),
        scratch_shapes=[
            pltpu.VMEM((2, size, 3 * size), BF16),
            pltpu.VMEM((2, 3 * size, size), BF16),
            pltpu.VMEM((2, size, size), F32),
            pltpu.VMEM((size, size), F32),
            pltpu.VMEM((NB, size), F32),
            pltpu.VMEM((NB, size), F32),
        ],
        compiler_params=pltpu.CompilerParams(vmem_limit_bytes=48 * 2**20),
        cost_estimate=pl.CostEstimate(flops=2 * 200 * size**3, bytes_accessed=2**22, transcendentals=0),
    )(flags_and_count, transition, update_map, quiet_root, observed_root, init_root)


def means_kernel(flags, quiet_map, seen_map, start, shares, out_ref, maps, maps_t, shifts, columns, lines):
    steps = shares.shape[0] * shares.shape[2]
    per, width = shares.shape[2], quiet_map.shape[0]
    for index, map_ref in enumerate((quiet_map, seen_map)):
        maps[index] = map_ref[...]
        maps_t[index] = map_ref[...].T
    shifts[...] = jnp.zeros_like(shifts)
    for block in range(shares.shape[0]):
        total = shares[block, 0]
        for part in range(1, shares.shape[1]):
            total = total + shares[block, part]
        shifts[block * per : (block + 1) * per, :] = total
    columns[...] = shifts[...].T
    lines[...] = jnp.zeros_like(lines)
    lane = lax.broadcasted_iota(jnp.int32, columns.shape, 1)
    row = start[...]
    column = None
    turned = jnp.zeros(columns.shape, F32)
    for t in range(steps):
        flag = jnp.where(flags[t] > 0, 1, 0)
        if t % 2 == 0:
            column = jnp.sum(maps[flag] * row, axis=1, keepdims=True) + columns[:, t : t + 1]
            turned = jnp.where(lane == t, column, turned)
        else:
            row = jnp.sum(maps_t[flag] * column, axis=0, keepdims=True) + shifts[t : t + 1, :]
            lines[t : t + 1, :] = row
    lines[...] = lines[...] + turned.T
    for block in range(shares.shape[0]):

        @pl.when(flags[steps] == (block + 1) * per)
        def _():
            out_ref[...] = lines[block * per : (block + 1) * per, :]


def means(flags_and_count, transition, update_map, init_mean, shares):
    size = transition.shape[0]
    steps = shares.shape[0] * shares.shape[2]
    padded = -(-steps // 128) * 128
    return pl.pallas_call(
        means_kernel,
        in_specs=[SMEM] + [VMEM] * 4,
        out_specs=VMEM,
        out_shape=jax.ShapeDtypeStruct((shares.shape[2], size), F32),
        scratch_shapes=[
            pltpu.VMEM((2, size, size), F32),
            pltpu.VMEM((2, size, size), F32),
            pltpu.VMEM((padded, size), F32),
            pltpu.VMEM((size, padded), F32),
            pltpu.VMEM((padded, size), F32),
        ],
        compiler_params=pltpu.CompilerParams(vmem_limit_bytes=48 * 2**20),
    )(flags_and_count, transition, update_map, init_mean[None], shares)


def local(frames, conv_taps, pooling, gain_matrix, transition, update_map, quiet_root, observed_root, init_mean, init_root, observed):
    step_count, channels, tile_rows, width = frames.shape
    reach = DILATION_STEP
    spaces = lax.axis_size("space")
    all_flags = lax.all_gather(observed, "tm", tiled=True)
    count = ((lax.axis_index("tm") + 1) * step_count).astype(jnp.int32)
    flags_and_count = jnp.concatenate([all_flags, count[None]])
    forward = [(i, i + 1) for i in range(spaces - 1)]
    backward = [(target, source) for source, target in forward]
    low = lax.ppermute(frames[:, :, tile_rows - reach :, :], "space", forward)
    high = lax.ppermute(frames[:, :, :reach, :], "space", backward)

    spread = jnp.pad(pooling, ((2 * reach, 2 * reach), (reach, reach)))
    pools = jnp.stack([
        spread[(1 - a) * reach : (1 - a) * reach + tile_rows + 2 * reach, (1 - b) * reach : (1 - b) * reach + width]
        for a in range(-1, 2)
        for b in range(-1, 2)
    ])
    grads, sums = moments(
        frames, pools[:, reach : reach + tile_rows], conv_taps, observed,
        lambda e: e, lambda r, c: r >= 0, tile_rows,
    )
    none = jnp.zeros((step_count, channels, reach, width), frames.dtype)
    edges = jnp.concatenate(
        [low, frames[:, :, : 2 * reach], none, frames[:, :, tile_rows - 2 * reach :], high, none], axis=2
    )
    flat = jnp.zeros((9, 3 * reach, width), F32)
    edge_pools = jnp.concatenate([pools[:, :reach], flat, flat[:, : 2 * reach], pools[:, reach + tile_rows :], flat[:, :reach]], axis=1)

    def position(e):
        return jnp.where(e < 4 * reach, e - reach, e + tile_rows - 6 * reach)

    def inside(r, c):
        same = (r < 4 * reach) == (c < 4 * reach)
        real = lambda e: lax.rem(e, 4 * reach) < 3 * reach
        halo = lambda e: (position(e) < 0) | (position(e) >= tile_rows)
        return same & real(r) & real(c) & (halo(r) | halo(c))

    edge_grads, edge_sums = moments(edges, edge_pools, conv_taps, observed, position, inside, tile_rows)
    weights = observed.astype(F32)
    gain_part = jnp.dot(sums + edge_sums, gain_matrix.T, precision=lax.Precision.HIGHEST, preferred_element_type=F32)
    gain_part = gain_part * weights[:, None]
    grad_local = (grads + edge_grads) / (tile_rows * spaces * width)
    shares = lax.all_gather(gain_part, ("tm", "space", "chan"))
    shares = shares.reshape(lax.axis_size("tm"), -1, step_count, transition.shape[0])
    tap_gradient = lax.psum(grad_local, "space")[None]
    roots = covariance(flags_and_count, transition, update_map, quiet_root, observed_root, init_root)
    filtered_means = means(flags_and_count, transition, update_map, init_mean, shares)
    return (filtered_means, roots[None], tap_gradient)


def solution(mesh):
    return jax.shard_map(
        local,
        mesh=mesh,
        in_specs=(
            P(("groups", "tm"), "chan", "space", None),
            P("chan", None),
            P("space", None),
            P(None, ("space", "chan")),
            P(),
            P(),
            P(),
            P(),
            P("groups"),
            P("groups", None),
            P(("groups", "tm")),
        ),
        out_specs=(
            P(("groups", "tm"), None),
            P(("groups", "tm"), None, None),
            P(("groups", "tm"), "chan", None),
        ),
        check_vma=False,
    )
```

time: 151 us -> 106 us (0.70)
  other arithmetic: 51.8 us -> 1.19 us
  matrix products: 44.4 us -> 0.08 us
  Pallas kernels: 0 us -> 31.6 us
  blocking collectives: 22.3 us -> 42.1 us
  between operations: 15.8 us -> 1.59 us
  local copies, waits for them, and re-layouts: 7.1 us -> 21.2 us
    dot_general x38 -> x1, matrix products: 43.9 us -> 0.08 us  [local(): jnp.dot(sums + edge_sums, gain_matrix.T, precision=lax.Precision.HIGHEST,...]
    another operation x7 -> x0, other arithmetic: 34.6 us -> none  [the longest x6 33.9 us: local(): block_roots = jnp.linalg.cholesky(final_state[2]).T[None]]
    pallas_call x0 -> x4, Pallas kernels: none -> 31.6 us  [the longest x1 18.3 us: covariance(): pl.pallas_call(covariance_kernel, in_specs=[SMEM] + [VMEM] * 5, out_specs...]
    all_gather x1, blocking collectives: 11.2 us -> 28.7 us  [local(): shares = lax.all_gather(gain_part, ('tm', 'space', 'chan'))]
    reduce_sum x1 -> x4, other arithmetic: 11.3 us -> 0.44 us  [the longest x2 0.25 us: moments(): grads = jnp.sum(grads.reshape(groups, 9, group, rows), axis=3)]
    unnamed x0 -> x1, blocking collectives: none -> 8.44 us
    unnamed x22 -> x33, local copies, waits for them, and re-layouts: 5.24 us -> 11.9 us
    psum x1 -> x0, blocking collectives: 6.1 us -> none  [local(): shifts = lax.psum(gain_part, ('space', 'chan'))]
  transfers between devices with their start and end apart: 4 -> 2, of which waited for: 1 -> 0; matrix products, arithmetic and copies ran while one was open for 24% -> 12% of each run, Pallas kernels for 0% -> 24%
where the time goes in v1:
time: 106 us; the launch traced here: 105 us
  blocking collectives  42.1 us (40%)
  Pallas kernels  31.6 us (30%)
  local copies, waits for them, and re-layouts  21.2 us (20%)
  starting transfers between devices  6.78 us (6%)
  between operations  1.59 us (2%)
  other arithmetic  1.19 us (1%)
    all_gather x1, blocking collectives, local(): shares = lax.all_gather(gain_part, ('tm', 'space', 'chan'))  28.7 us
    pallas_call x1, Pallas kernels, covariance(): pl.pallas_call(covariance_kernel, in_specs=[SMEM] + [VMEM] * 5, out_specs...  18.3 us
    unnamed x33, local copies, waits for them, and re-layouts  11.9 us
    pallas_call x2, Pallas kernels, moments(): pl.pallas_call(functools.partial(moments_kernel, rows, group, position, i...  10.1 us
    unnamed x1, blocking collectives  8.44 us
    ppermute x1, starting transfers between devices, local(): low = lax.ppermute(frames[:, :, tile_rows - reach:, :], 'space', forward)  5.5 us
    psum x1, blocking collectives, local(): tap_gradient = lax.psum(grad_local, 'space')[None]  4.98 us
    concatenate x1, local copies, waits for them, and re-layouts, local(): jnp.concatenate([low, frames[:, :, :2 * reach], none, frames[:, :, tile_r...  3.89 us
  transfers between devices with their start and end apart: 2, of which 0 were waited for; matrix products, arithmetic and copies ran while one was open for 12% of the time, Pallas kernels for 24%

profile of v1, /device:TPU:0, one launch (start us, length us, event | category | flops | bytes accessed | tf_op | source)
XLA Modules:
  0.0 104.6 jit_solution(10232023744224077358)
XLA Ops:
  0.7 2.3 %fusion.20 = (bf16[4,32,2,256]{3,2,1,0:T(2,128)(2,1)}, bf16[4,32,2,256]{3,2,1,0:T(2,128)(2,1)}) fusion(bf16[4,32,32,256]{3,2,1,0:T(8,128)(2,1)} %x_ref.1), kind=kLoop, calls=%fused_computation.32 | loop fusion | bytes 524288 | tf_op jit(solution)/shard_map/slice | solution.py:274
  2.9 5.5 %collective-permute-start = (bf16[4,32,2,256]{3,2,1,0:T(2,128)(2,1)}, bf16[4,32,2,256]{3,2,1,0:T(2,128)(2,1)}, u32[]{:S(2)}, u32[]{:S(2)}) collective-permute-start(bf16[4,32,2,256]{3,2,1,0:T(2,128)(2,1)} %get-tuple-element.18), channel_id=1, source_target_pairs={{0,2},{1,3},{4,6},{5,7},{8,10},{9,11},{12,14},{13,15},{16,18},{17,... | collective-permute-start | bytes 393224 | tf_op jit(solution)/shard_map/ppermute | solution.py:273
  8.4 1.3 %collective-permute-start.1 = (bf16[4,32,2,256]{3,2,1,0:T(2,128)(2,1)}, bf16[4,32,2,256]{3,2,1,0:T(2,128)(2,1)}, u32[]{:S(2)}, u32[]{:S(2)}) collective-permute-start(bf16[4,32,2,256]{3,2,1,0:T(2,128)(2,1)} %get-tuple-element.17), channel_id=1, source_target_pairs={{2,0},{3,1},{6,4},{7,5},{10,8},{11,9},{14,12},{15,13},{18,16},{19,... | collective-permute-start | bytes 393224 | tf_op jit(solution)/shard_map/ppermute | solution.py:274
  9.7 0.8 fusion.2
  10.5 0.8 fusion.4
  11.3 0.8 fusion.6
  12.1 0.8 fusion.8
  13.8 0.8 fusion.12
  14.6 0.8 fusion.14
  16.2 0.8 fusion.18
  17.8 1.2 %dynamic-slice = u32[1]{0:T(128)} dynamic-slice(u32[32]{0:T(128)} %constant.27, u32[]{:T(128)S(6)} %add.16), dynamic_slice_sizes={1} | dynamic-slice | bytes 12
  19.7 0.9 dynamic-update-slice
  20.5 8.4 %all-reduce.1 = s32[16]{0:T(128)S(1)} all-reduce(s32[16]{0:T(128)S(1)} %dynamic-update-slice), channel_id=1, replica_groups=mesh['groups'=2,'tm'=4,'space'=2,'chan'=2] {'tm'}, use_global_device_ids=true, to_apply=%add.1 | all-reduce | flops 16 | bytes 128
  28.9 0.8 copy.25.taps
  29.7 0.8 broadcast_in_dim.27
  30.7 6.4 %shard_map.130 = (f32[4,9,256]{2,1,0:T(8,128)S(1)}, f32[4,32,256]{2,1,0:T(8,128)S(1)}) custom-call(s32[4]{0:T(128)S(1)} %copy-done.8, f32[32,9]{1,0:T(8,128)S(1)} %copy.25.taps, bf16[4,32,32,256]{3,2,1,0:T(8,128)(2,1)S(1)} %copy-done.1, f32[9,32,256]{2,1,0:T(8,128)S(1)} %slice.72.pools, f32[9,1024]{1,0:T(8,128)S(1)} %reshape.40.taps_wide), custom_call_target="tpu_custom_call" | custom-call | flops 2684354560 | bytes 2097152 | tf_op jit(solution)/shard_map/pallas_call | solution.py:82
  38.2 0.9 copy-done.6
  39.2 0.9 copy-done.7
  40.1 18.3 %shard_map.133 = f32[256,256]{1,0:T(8,128)} custom-call(s32[17]{0:T(128)S(1)} %pad_add_fusion.flags, f32[256,256]{1,0:T(8,128)S(1)} %copy-done.2, f32[256,256]{1,0:T(8,128)S(1)} %copy-done.3, f32[256,256]{1,0:T(8,128)S(1)} %copy-done.5, f32[256,256]{1,0:T(8,128)S(1)} %copy-done.6, f32[256,256]{1,0:T(8,128)S(1)} %copy-done.7), custom_call_target="tpu_custom_call" | custom-call | flops 6710886400 | bytes 4194304 | tf_op jit(solution)/shard_map/pallas_call | solution.py:192
  58.7 3.9 %concatenate.10.x_ref = bf16[4,32,16,256]{3,2,1,0:T(8,128)(2,1)S(1)} concatenate(bf16[4,32,2,256]{3,2,1,0:T(2,128)(2,1)} %collective-permute-done, bf16[4,32,4,256]{3,2,1,0:T(4,128)(2,1)S(1)} %get-tuple-element.20, bf16[4,32,2,256]{3,2,1,0:T(2,128)(2,1)S(1)} %broadcast_in_dim.28, bf16[4,32,4,256]{3,2,1,0:T(4,128)(2,1)S(1)} %get-tuple-element.19, ...), dimensions={2} | concatenate | bytes 2097152 | tf_op jit(solution)/shard_map/concatenate | solution.py:287
  62.6 3.7 %shard_map.131 = (f32[2,9,256]{2,1,0:T(8,128)S(1)}, f32[2,64,256]{2,1,0:T(8,128)S(1)}) custom-call(s32[4]{0:T(128)S(1)} %copy-done.8, f32[32,9]{1,0:T(8,128)S(1)} %copy.25.taps, bf16[4,32,16,256]{3,2,1,0:T(8,128)(2,1)S(1)} %concatenate.10.x_ref, f32[9,16,256]{2,1,0:T(8,128)S(1)} %concatenate.11.pools, f32[9,512]{1,0:T(8,128)S(1)} %reshape.43.taps_wide), custom_call_target="tpu_custom_call" | custom-call | flops 1342177280 | bytes 1048576 | tf_op jit(solution)/shard_map/pallas_call | solution.py:82
  66.7 28.7 %all-gather.1 = f32[16,4,256]{2,1,0:T(4,128)S(1)} all-gather(f32[1,4,256]{2,1,0:T(4,128)S(1)} %fusion), channel_id=2, replica_groups=mesh['groups'=2,'tm'=4,'space'=2,'chan'=2] {'tm','space','chan'}, dimensions={0}, use_global_device_ids=true | all-gather | bytes 69632 | tf_op jit(solution)/shard_map/all_gather | solution.py:307
  95.8 5.0 %psum.7 = f32[1,32,9]{1,2,0:T(8,128)S(1)} all-reduce(f32[1,32,9]{1,2,0:T(8,128)S(1)} %multiply_bitcast_fusion), channel_id=1, replica_groups=mesh['groups'=2,'tm'=4,'space'=2,'chan'=2] {'space'}, use_global_device_ids=true, to_apply=%region_4.5 | all-reduce | flops 288 | bytes 2304 | tf_op jit(solution)/shard_map/psum | solution.py:309
  101.3 3.2 %shard_map.132 = f32[4,256]{1,0:T(4,128)} custom-call(s32[17]{0:T(128)S(1)} %pad_add_fusion.flags, f32[256,256]{1,0:T(8,128)S(1)} %copy-done.2, f32[256,256]{1,0:T(8,128)S(1)} %copy-done.3, f32[1,256]{1,0:T(1,128)S(1)} %bitcast.60, f32[4,4,4,256]{3,2,1,0:T(4,128)S(1)} %bitcast.59), custom_call_target="tpu_custom_call" | custom-call | tf_op jit(solution)/shard_map/pallas_call | solution.py:248
  (55 shorter events, 5.0 us)
Async XLA Ops:
  0.6 66.0 %copy-start = (f32[256,32]{0,1:T(8,128)S(1)}, f32[256,32]{0,1:T(8,128)}, u32[]{:S(2)}) copy-start(f32[256,32]{0,1:T(8,128)} %param.14) | copy-start | bytes 98308
  0.6 30.0 %copy-start.1 = (bf16[4,32,32,256]{3,2,1,0:T(8,128)(2,1)S(1)}, bf16[4,32,32,256]{3,2,1,0:T(8,128)(2,1)}, u32[]{:S(2)}) copy-start(bf16[4,32,32,256]{3,2,1,0:T(8,128)(2,1)} %x_ref.1) | copy-start | bytes 6291460
  0.7 30.0 %copy-start.8 = (s32[4]{0:T(128)S(1)}, s32[4]{0:T(128)}, u32[]{:S(2)}) copy-start(s32[4]{0:T(128)} %flags.3) | copy-start | bytes 52
  2.9 55.7 %collective-permute-start = (bf16[4,32,2,256]{3,2,1,0:T(2,128)(2,1)}, bf16[4,32,2,256]{3,2,1,0:T(2,128)(2,1)}, u32[]{:S(2)}, u32[]{:S(2)}) collective-permute-start(bf16[4,32,2,256]{3,2,1,0:T(2,128)(2,1)} %get-tuple-element.18), channel_id=1, source_target_pairs={{0,2},{1,3},{4,6},{5,7},{8,10},{9,11},{12,14},{13,15},{16,18},{17,... | collective-permute-start | bytes 393224 | tf_op jit(solution)/shard_map/ppermute | solution.py:273
  8.4 50.2 %collective-permute-start.1 = (bf16[4,32,2,256]{3,2,1,0:T(2,128)(2,1)}, bf16[4,32,2,256]{3,2,1,0:T(2,128)(2,1)}, u32[]{:S(2)}, u32[]{:S(2)}) collective-permute-start(bf16[4,32,2,256]{3,2,1,0:T(2,128)(2,1)} %get-tuple-element.17), channel_id=1, source_target_pairs={{2,0},{3,1},{6,4},{7,5},{10,8},{11,9},{14,12},{15,13},{18,16},{19,... | collective-permute-start | bytes 393224 | tf_op jit(solution)/shard_map/ppermute | solution.py:274
  30.7 6.7 %copy-start.9 = (f32[32,9]{0,1:T(8,128)S(1)}, f32[32,9]{0,1:T(8,128)}, u32[]{:S(2)}) copy-start(f32[32,9]{0,1:T(8,128)} %param.12) | copy-start | bytes 3460
  30.7 7.5 %copy-start.2 = (f32[256,256]{1,0:T(8,128)S(1)}, f32[256,256]{1,0:T(8,128)}, u32[]{:S(2)}) copy-start(f32[256,256]{1,0:T(8,128)} %quiet_map.3) | copy-start | bytes 786436
  30.7 7.5 %copy-start.3 = (f32[256,256]{1,0:T(8,128)S(1)}, f32[256,256]{1,0:T(8,128)}, u32[]{:S(2)}) copy-start(f32[256,256]{1,0:T(8,128)} %seen_map.3) | copy-start | bytes 786436
  30.7 7.5 %copy-start.5 = (f32[256,256]{1,0:T(8,128)S(1)}, f32[256,256]{1,0:T(8,128)}, u32[]{:S(2)}) copy-start(f32[256,256]{1,0:T(8,128)} %quiet_root.1) | copy-start | bytes 786436
  38.2 1.0 copy-start.6
  39.2 0.9 copy-start.7
  62.6 38.7 %copy-start.4 = (f32[256]{0:T(256)S(1)}, f32[256]{0:T(256)}, u32[]{:S(2)}) copy-start(f32[256]{0:T(256)} %param.19) | copy-start | bytes 3076

commit v2 on v1

v2 whole, which is shorter than its diff:
```python
import functools

import jax
import jax.numpy as jnp
from jax import lax
from jax.experimental import pallas as pl
from jax.experimental.pallas import tpu as pltpu
from jax.sharding import PartitionSpec as P

DILATION_STEP = 2
NB = 16
F32 = jnp.float32
BF16 = jnp.bfloat16
VMEM = pl.BlockSpec(memory_space=pltpu.VMEM)
SMEM = pl.BlockSpec(memory_space=pltpu.SMEM)

NT_DIMS = (((1,), (1,)), ((), ()))
TN_DIMS = (((0,), (0,)), ((), ()))
PAIRS = (((0, 0), 0), ((1, 1), 1), ((-1, -1), 2), ((0, 1), 3), ((-1, 0), 3), ((-1, 1), 4))


MESH = pl.DeviceIdType.MESH


def fold_grads(grads, kind, gram, rows, group, owner, row_h, col_h, allowed, limit, wide):
    folded = jnp.zeros((rows, group * rows), F32)
    for c in range(group):
        folded = jnp.where(owner == c, gram[c * rows : (c + 1) * rows, :], folded)
    for a in range(-1, 2):
        for z in range(-1, 2):
            h = row_h - DILATION_STEP * a
            keep = (h >= 0) & (h < limit) & (row_h - col_h == DILATION_STEP * (a - z)) & allowed
            row = jnp.sum(jnp.where(keep, folded, 0.0), axis=0, keepdims=True)
            for (b, y), which in PAIRS:
                if which != kind:
                    continue
                k, q = 3 * (a + 1) + b + 1, 3 * (z + 1) + y + 1
                grads[k] = grads[k] + row * wide[q]
                if b != y:
                    grads[q] = grads[q] + row * wide[k]


def gram_grads(blocks, flags, wide, rows, group, row_h, col_h, allowed, limit):
    size, width = blocks[0].shape
    reach = DILATION_STEP
    lane = lax.broadcasted_iota(jnp.int32, (size, width), 1)
    left, low, high, one, two = [], [], [], [], []
    for t, block in enumerate(blocks):
        x = block.astype(F32)
        scaled = x * flags[t]
        left.append(scaled.astype(BF16))
        low.append(jnp.where(lane >= reach, scaled, 0.0).astype(BF16))
        high.append(jnp.where(lane < width - reach, scaled, 0.0).astype(BF16))
        one.append(jnp.where(lane < width - reach, pltpu.roll(x, width - reach, 1), 0.0).astype(BF16))
        two.append(jnp.where(lane < width - 2 * reach, pltpu.roll(x, width - 2 * reach, 1), 0.0).astype(BF16))
    cat = lambda pieces: jnp.concatenate(pieces, axis=1)
    left, plain = cat(left), cat(blocks)
    owner = lax.div(lax.broadcasted_iota(jnp.int32, (rows, size), 1), rows)
    grads = [jnp.zeros((1, size), F32) for _ in range(9)]
    for kind, (lhs, rhs) in enumerate(((left, plain), (cat(low), plain), (cat(high), plain), (left, cat(one)), (left, cat(two)))):
        gram = lax.dot_general(lhs, rhs, NT_DIMS, preferred_element_type=F32)
        fold_grads(grads, kind, gram, rows, group, owner, row_h, col_h, allowed, limit, wide)
    return grads


def observe_kernel(sizes, flags, taps, x_ref, pooling, gains, shift_ref, flag_ref, grad_ref,
                   tops, bottoms, lows, highs, pools, sums, grads_all, slots, grad_slots,
                   halo_send, halo_recv, send_sem, recv_sem, grad_send, grad_recv):
    n_tm, n_space, n_chan = sizes
    steps, channels, rows, width = x_ref.shape
    reach = DILATION_STEP
    group = min(channels, 256 // rows)
    groups = channels // group
    size = group * rows
    pack = group * reach
    n_all = n_tm * n_space * n_chan
    tm, space, chan = lax.axis_index("tm"), lax.axis_index("space"), lax.axis_index("chan")
    me = (tm * n_space + space) * n_chan + chan

    def place(p):
        return {"tm": lax.div(p, n_space * n_chan), "space": lax.rem(lax.div(p, n_chan), n_space), "chan": lax.rem(p, n_chan)}

    barrier = pltpu.get_barrier_semaphore()

    def greet(i, carry):
        pl.semaphore_signal(barrier, inc=1, device_id=place(lax.rem(me + i, n_all)), device_id_type=MESH)
        return carry

    lax.fori_loop(1, n_all, greet, 0)

    def pick(count, first_row):
        r = lax.broadcasted_iota(jnp.int32, (count, size), 0)
        c = lax.broadcasted_iota(jnp.int32, (count, size), 1)
        return jnp.where(c == lax.div(r, reach) * rows + lax.rem(r, reach) + first_row, 1.0, 0.0).astype(BF16)

    pick_top, pick_bottom = pick(pack, 0), pick(pack, rows - reach)
    for t in range(steps):
        for g in range(groups):
            x = x_ref[t, g * group : (g + 1) * group].reshape(size, width)
            at = pl.ds((g * steps + t) * pack, pack)
            tops[at, :] = jnp.dot(pick_top, x, preferred_element_type=F32).astype(BF16)
            bottoms[at, :] = jnp.dot(pick_bottom, x, preferred_element_type=F32).astype(BF16)
    pl.semaphore_wait(barrier, n_all - 1)
    down = pltpu.make_async_remote_copy(
        src_ref=bottoms, dst_ref=lows, send_sem=halo_send.at[0], recv_sem=halo_recv.at[0],
        device_id={"space": lax.rem(space + 1, n_space)}, device_id_type=MESH)
    up = pltpu.make_async_remote_copy(
        src_ref=tops, dst_ref=highs, send_sem=halo_send.at[1], recv_sem=halo_recv.at[1],
        device_id={"space": lax.rem(space + n_space - 1, n_space)}, device_id_type=MESH)
    has_next, has_last = space < n_space - 1, space > 0

    @pl.when(has_next)
    def _():
        down.start()

    @pl.when(has_last)
    def _():
        up.start()

    pool = pooling[...]
    row_i = lax.broadcasted_iota(jnp.int32, (rows, width), 0)
    lane_i = lax.broadcasted_iota(jnp.int32, (rows, width), 1)
    for b in range(-1, 2):
        moved = pool
        if b:
            moved = pltpu.roll(pool, (reach * b) % width, 1)
            moved = jnp.where((lane_i >= reach * b) & (lane_i < width + reach * b), moved, 0.0)
        for a in range(-1, 2):
            turned = moved
            if a:
                turned = pltpu.roll(moved, (reach * a) % rows, 0)
                turned = jnp.where((row_i >= reach * a) & (row_i < rows + reach * a), turned, 0.0)
            pools[3 * (a + 1) + b + 1] = turned
    flag_values = [flags[t].astype(F32) for t in range(steps)]

    def widened(first, count, each):
        owner = lax.div(lax.broadcasted_iota(jnp.int32, (1, count * each), 1), each)
        wide = []
        for k in range(9):
            row = jnp.zeros((1, count * each), F32)
            for c in range(count):
                row = jnp.where(owner == c, taps[first + c, k], row)
            wide.append(row)
        return wide

    def reduced(grads, first, count, each):
        stack = jnp.concatenate(grads + [jnp.zeros((7, count * each), F32)], axis=0)
        r = lax.broadcasted_iota(jnp.int32, (count * each, 128), 0)
        c = lax.broadcasted_iota(jnp.int32, (count * each, 128), 1)
        ones = jnp.where(c == first + lax.div(r, each), 1.0, 0.0).astype(BF16)
        h, m, l = split3(stack)
        dot = lambda part: jnp.dot(part, ones, preferred_element_type=F32)
        return dot(h) + (dot(m) + dot(l))

    grads_all[...] = jnp.zeros_like(grads_all)
    row_e = lax.broadcasted_iota(jnp.int32, (rows, size), 0)
    col_e = lax.rem(lax.broadcasted_iota(jnp.int32, (rows, size), 1), rows)

    def interior(g, carry):
        first = g * group
        for c in range(group):
            weight = taps[first + c, 0] * pools[0]
            for k in range(1, 9):
                weight = weight + taps[first + c, k] * pools[k]
            for t in range(steps):
                part = x_ref[t, first + c].astype(F32) * weight
                sums[t, pl.ds(first + c, 1), :] = jnp.sum(part, axis=0, keepdims=True)
        blocks = [x_ref[t, pl.ds(first, group)].reshape(size, width) for t in range(steps)]
        grads = gram_grads(blocks, flag_values, widened(first, group, rows), rows, group, row_e, col_e, row_e >= 0, rows)
        grads_all[...] += reduced(grads, first, group, rows)
        return carry

    lax.fori_loop(0, groups, interior, 0)

    @pl.when(has_last)
    def _():
        up.wait_send()
        down.wait_recv()

    @pl.when(has_next)
    def _():
        down.wait_send()
        up.wait_recv()

    edge = 8 * reach
    half = group * edge
    r = lax.broadcasted_iota(jnp.int32, (half, size), 0)
    c = lax.broadcasted_iota(jnp.int32, (half, size), 1)
    e = lax.rem(r, edge)

    def position(e):
        return jnp.where(e < 4 * reach, e - reach, e + rows - 6 * reach)

    def real(e):
        return lax.rem(e, 4 * reach) < 3 * reach

    def halo(e):
        return (position(e) < 0) | (position(e) >= rows)

    own = jnp.where(real(e) & ~halo(e) & (c == lax.div(r, edge) * rows + position(e)), 1.0, 0.0).astype(BF16)
    r = lax.broadcasted_iota(jnp.int32, (half, pack), 0)
    c = lax.broadcasted_iota(jnp.int32, (half, pack), 1)
    e = lax.rem(r, edge)
    from_low = jnp.where((e < reach) & (c == lax.div(r, edge) * reach + e), 1.0, 0.0).astype(BF16)
    from_high = jnp.where((e >= 6 * reach) & (e < 7 * reach) & (c == lax.div(r, edge) * reach + e - 6 * reach), 1.0, 0.0).astype(BF16)
    edge_row = lax.broadcasted_iota(jnp.int32, (edge, width), 0)
    edge_pools = []
    for b in range(3):
        shifted = pools[3 + b]
        low_part = jnp.where(edge_row < reach, shifted[0:edge, :], 0.0)
        high_part = jnp.where((edge_row >= 6 * reach) & (edge_row < 7 * reach), pltpu.roll(shifted[rows - edge : rows, :], edge - reach, 0), 0.0)
        edge_pools.append((low_part, high_part))
    many = 2 * group
    e_row = lax.broadcasted_iota(jnp.int32, (edge, many * edge), 0)
    e_col = lax.rem(lax.broadcasted_iota(jnp.int32, (edge, many * edge), 1), edge)
    allowed = ((e_row < 4 * reach) == (e_col < 4 * reach)) & real(e_row) & real(e_col) & (halo(e_row) | halo(e_col))

    def outer(v, carry):
        blocks = []
        for t in range(steps):
            halves = []
            for q in range(2):
                g = 2 * v + q
                x = x_ref[t, pl.ds(g * group, group)].reshape(size, width)
                at = pl.ds(pl.multiple_of((g * steps + t) * pack, pack), pack)
                low_rows = jnp.where(has_last, lows[at, :].astype(F32), 0.0).astype(BF16)
                high_rows = jnp.where(has_next, highs[at, :].astype(F32), 0.0).astype(BF16)
                dot = lambda m, y: jnp.dot(m, y, preferred_element_type=F32)
                halves.append(dot(own, x) + dot(from_low, low_rows) + dot(from_high, high_rows))
            blocks.append(jnp.concatenate(halves, axis=0))
        first = v * many
        for i in range(many):
            weight = jnp.zeros((edge, width), F32)
            for b in range(3):
                low_part, high_part = edge_pools[b]
                weight = weight + taps[first + i, b] * low_part + taps[first + i, 6 + b] * high_part
            for t in range(steps):
                part = blocks[t][i * edge : (i + 1) * edge, :] * weight
                at = pl.ds(first + i, 1)
                sums[t, at, :] = sums[t, at, :] + jnp.sum(part, axis=0, keepdims=True)
        grads = gram_grads([y.astype(BF16) for y in blocks], flag_values, widened(first, many, edge), edge, many, position(e_row), position(e_col), allowed, rows)
        grads_all[...] += reduced(grads, first, many, edge)
        return carry

    lax.fori_loop(0, groups // 2, outer, 0)

    scale = 1.0 / (rows * n_space * width)
    grad_slots[space] = grads_all[...] * scale
    for t in range(steps):
        tile = jnp.sum(sums[t], axis=1, keepdims=True)
        share = jnp.sum(tile * gains[...], axis=0, keepdims=True) * flag_values[t]
        slots[me, pl.ds(t, 1), :] = share
        slots[me, pl.ds(steps + t, 1), :] = jnp.zeros((1, share.shape[1]), F32) + flag_values[t]

    def share_copy(p, slot):
        return pltpu.make_async_remote_copy(
            src_ref=slots.at[slot], dst_ref=slots.at[slot], send_sem=send_sem.at[p], recv_sem=recv_sem.at[slot],
            device_id=place(p), device_id_type=MESH)

    def grad_copy(s, slot):
        return pltpu.make_async_remote_copy(
            src_ref=grad_slots.at[slot], dst_ref=grad_slots.at[slot], send_sem=grad_send.at[s], recv_sem=grad_recv.at[slot],
            device_id={"space": s}, device_id_type=MESH)

    def each(count, mine, act):
        def turn(i, carry):
            act(lax.rem(mine + i, count))
            return carry

        lax.fori_loop(1, count, turn, 0)

    each(n_all, me, lambda p: share_copy(p, me).start())
    each(n_space, space, lambda s: grad_copy(s, space).start())
    each(n_all, me, lambda p: share_copy(p, p).wait_recv())
    each(n_space, space, lambda s: grad_copy(s, s).wait_recv())
    for block in range(n_tm):
        total = slots[block * n_space * n_chan, 0:steps, :]
        for part in range(1, n_space * n_chan):
            total = total + slots[block * n_space * n_chan + part, 0:steps, :]
        shift_ref[block * steps : (block + 1) * steps, :] = total
        marks = slots[block * n_space * n_chan, steps : 2 * steps, 0:128]
        flag_ref[block * steps : (block + 1) * steps, :] = jnp.where(marks > 0.5, 1, 0)
    total = grad_slots[0]
    for part in range(1, n_space):
        total = total + grad_slots[part]
    grad_ref[...] = total[0:9, 0:channels]
    each(n_all, me, lambda p: share_copy(p, me).wait_send())
    each(n_space, space, lambda s: grad_copy(s, space).wait_send())


def observe(flags, taps, frames, pooling, gains):
    steps, channels, rows, width = frames.shape
    states = gains.shape[1]
    sizes = tuple(lax.axis_size(name) for name in ("tm", "space", "chan"))
    n_all = sizes[0] * sizes[1] * sizes[2]
    packed = steps * channels * DILATION_STEP
    return pl.pallas_call(
        functools.partial(observe_kernel, sizes),
        in_specs=[SMEM, SMEM, VMEM, VMEM, VMEM],
        out_specs=[VMEM] * 3,
        out_shape=[
            jax.ShapeDtypeStruct((sizes[0] * steps, states), F32),
            jax.ShapeDtypeStruct((sizes[0] * steps, 128), jnp.int32),
            jax.ShapeDtypeStruct((9, channels), F32),
        ],
        scratch_shapes=[pltpu.VMEM((packed, width), BF16)] * 4 + [
            pltpu.VMEM((9, rows, width), F32),
            pltpu.VMEM((steps, channels, width), F32),
            pltpu.VMEM((16, 128), F32),
            pltpu.VMEM((n_all, 2 * steps, states), F32),
            pltpu.VMEM((sizes[1], 16, 128), F32),
            pltpu.SemaphoreType.DMA((2,)),
            pltpu.SemaphoreType.DMA((2,)),
            pltpu.SemaphoreType.DMA((n_all,)),
            pltpu.SemaphoreType.DMA((n_all,)),
            pltpu.SemaphoreType.DMA((sizes[1],)),
            pltpu.SemaphoreType.DMA((sizes[1],)),
        ],
        compiler_params=pltpu.CompilerParams(collective_id=0, has_side_effects=True, vmem_limit_bytes=48 * 2**20),
    )(flags, taps, frames, pooling, gains)


def split2(x):
    high = x.astype(BF16)
    return high, (x - high.astype(F32)).astype(BF16)


def split3(x):
    high = x.astype(BF16)
    rest = x - high.astype(F32)
    mid = rest.astype(BF16)
    return high, mid, (rest - mid.astype(F32)).astype(BF16)


def gram3(x):
    h, m, l = split3(x)
    lhs = jnp.concatenate([h, h, m, h, l, m], axis=0)
    rhs = jnp.concatenate([h, m, h, l, h, m], axis=0)
    return lax.dot_general(lhs, rhs, TN_DIMS, preferred_element_type=F32)


def mean_chain(per, tm, flags, quiet_map, seen_map, start, shift_ref, out_ref, maps, maps_t, shifts, columns, lines):
    steps = shift_ref.shape[0]
    for index, map_ref in enumerate((quiet_map, seen_map)):
        maps[index] = map_ref[...]
        maps_t[index] = map_ref[...].T
    shifts[...] = jnp.zeros_like(shifts)
    shifts[0:steps, :] = shift_ref[...]
    columns[...] = shifts[...].T
    lines[...] = jnp.zeros_like(lines)
    lane = lax.broadcasted_iota(jnp.int32, columns.shape, 1)
    row = start[...]
    column = None
    turned = jnp.zeros(columns.shape, F32)
    for t in range(steps):
        flag = flags[t, 0]
        if t % 2 == 0:
            column = jnp.sum(maps[flag] * row, axis=1, keepdims=True) + columns[:, t : t + 1]
            turned = jnp.where(lane == t, column, turned)
        else:
            row = jnp.sum(maps_t[flag] * column, axis=0, keepdims=True) + shifts[t : t + 1, :]
            lines[t : t + 1, :] = row
    lines[...] = lines[...] + turned.T
    for block in range(steps // per):

        @pl.when(tm == block)
        def _():
            out_ref[...] = lines[block * per : (block + 1) * per, :]


def state_kernel(per, flags, quiet_map, seen_map, quiet_root, seen_root, init_root, start_mean, shift_ref, out_ref, mean_ref, maps, maps_t, grams, cov, panel, held, plain, plain_t, shifts, columns, lines):
    size = out_ref.shape[0]
    tm = lax.axis_index("tm")
    mean_chain(per, tm, flags, quiet_map, seen_map, start_mean, shift_ref, mean_ref, plain, plain_t, shifts, columns, lines)
    for index, (map_ref, root_ref) in enumerate(((quiet_map, quiet_root), (seen_map, seen_root))):
        h, l = split2(map_ref[...])
        maps[index] = jnp.concatenate([h, h, l], axis=1)
        h, l = split2(map_ref[...].T)
        maps_t[index] = jnp.concatenate([h, h, l], axis=0)
        grams[index] = gram3(root_ref[...])
    cov[...] = gram3(init_root[...])

    def advance(t, carry):
        flag = flags[t, 0]
        h, l = split2(cov[...])
        moved = jnp.dot(maps[flag], jnp.concatenate([h, l, h], axis=0), preferred_element_type=F32)
        h, l = split2(moved)
        cov[...] = jnp.dot(jnp.concatenate([h, l, h], axis=1), maps_t[flag], preferred_element_type=F32) + grams[flag]
        return carry

    lax.fori_loop(0, (tm + 1) * per, advance, 0)

    lane = lax.broadcasted_iota(jnp.int32, (8, size), 1)
    held[...] = jnp.zeros_like(held)
    panel[...] = cov[0:NB, :]

    def block(b, carry):
        start = pl.multiple_of(b * NB, NB)
        before = held[...]
        rows = panel[...]
        corner = pltpu.roll(rows, lax.rem(size - start, size), 1)[:, 0:128]
        wide = [jnp.broadcast_to(corner[:, k : k + 1], (NB, 128)) for k in range(NB)]
        d = [[None] * NB for _ in range(NB)]
        for k in range(NB):
            for i in range(k + 1):
                d[i][k] = jnp.broadcast_to(wide[k][i : i + 1, :], (8, 128))
        lines = [jnp.broadcast_to(panel[i : i + 1, :], (8, size)) for i in range(NB)]
        for j in range(NB):
            r = lax.rsqrt(d[j][j])
            r = r * (1.5 - 0.5 * d[j][j] * r * r)
            u = {k: d[j][k] * r for k in range(j + 1, NB)}
            twice = jnp.concatenate([r] * (size // 128), axis=1)
            line = jnp.where(lane >= start + j, lines[j] * twice, 0.0)
            held[j : j + 1, :] = line[0:1, :]
            for i in range(j + 1, NB):
                lines[i] = lines[i] - jnp.concatenate([u[i]] * (size // 128), axis=1) * line
                for k in range(i, NB):
                    d[i][k] = d[i][k] - u[i] * u[k]
        cov[...] = cov[...] - gram3(before)
        done = held[...]
        out_ref[pl.ds(start, NB), :] = done
        after = lax.rem(start + NB, size)
        turned = pltpu.roll(done, lax.rem(size - after, size), 1)[:, 0:128]
        h, m, l = split3(done)
        p, q, s = split3(turned)
        lhs = jnp.concatenate([p, p, q, p, s, q], axis=0)
        rhs = jnp.concatenate([h, m, h, l, h, m], axis=0)
        change = lax.dot_general(lhs, rhs, TN_DIMS, preferred_element_type=F32)
        panel[...] = cov[pl.ds(pl.multiple_of(after, NB), NB), :] - change[0:NB, :]
        return carry

    lax.fori_loop(0, size // NB, block, 0)


def state(per, flags, transition, update_map, quiet_root, observed_root, init_root, init_mean, shifts):
    size = transition.shape[0]
    steps = shifts.shape[0]
    padded = -(-steps // 128) * 128
    return pl.pallas_call(
        functools.partial(state_kernel, per),
        in_specs=[SMEM] + [VMEM] * 7,
        out_specs=[VMEM] * 2,
        out_shape=[jax.ShapeDtypeStruct((size, size), F32), jax.ShapeDtypeStruct((per, size), F32)],
        scratch_shapes=[
            pltpu.VMEM((2, size, 3 * size), BF16),
            pltpu.VMEM((2, 3 * size, size), BF16),
            pltpu.VMEM((2, size, size), F32),
            pltpu.VMEM((size, size), F32),
            pltpu.VMEM((NB, size), F32),
            pltpu.VMEM((NB, size), F32),
            pltpu.VMEM((2, size, size), F32),
            pltpu.VMEM((2, size, size), F32),
            pltpu.VMEM((padded, size), F32),
            pltpu.VMEM((size, padded), F32),
            pltpu.VMEM((padded, size), F32),
        ],
        compiler_params=pltpu.CompilerParams(vmem_limit_bytes=48 * 2**20),
    )(flags, transition, update_map, quiet_root, observed_root, init_root, init_mean[None], shifts)


def local(frames, conv_taps, pooling, gain_matrix, transition, update_map, quiet_root, observed_root, init_mean, init_root, observed):
    per = frames.shape[0]
    shifts, flags, tap_gradient = observe(observed, conv_taps, frames, pooling, gain_matrix.T)
    roots, filtered_means = state(per, flags, transition, update_map, quiet_root, observed_root, init_root, init_mean, shifts)
    return (filtered_means, roots[None], tap_gradient.T[None])


def solution(mesh):
    return jax.shard_map(
        local,
        mesh=mesh,
        in_specs=(
            P(("groups", "tm"), "chan", "space", None),
            P("chan", None),
            P("space", None),
            P(None, ("space", "chan")),
            P(),
            P(),
            P(),
            P(),
            P("groups"),
            P("groups", None),
            P(("groups", "tm")),
        ),
        out_specs=(
            P(("groups", "tm"), None),
            P(("groups", "tm"), None, None),
            P(("groups", "tm"), "chan", None),
        ),
        check_vma=False,
    )
```

time: 106 us -> 53.1 us (0.50)
  the two profiles are of different devices: /device:TPU:0 before, /device:TPU:27 now
where the time goes in v2:
time: 53.1 us; the launch traced here: 52.8 us
  Pallas kernels  46.9 us (88%)
  local copies, waits for them, and re-layouts  5.17 us (10%)
  between operations  0.68 us (1%)
    pallas_call x1, Pallas kernels, state(): pl.pallas_call(functools.partial(state_kernel, per), in_specs=[SMEM] + [V...  27.8 us
    pallas_call x1, Pallas kernels, observe(): pl.pallas_call(functools.partial(observe_kernel, sizes), in_specs=[SMEM,...  19.1 us
    unnamed x22, local copies, waits for them, and re-layouts  5.17 us

profile of v2, /device:TPU:27, one launch (start us, length us, event | category | flops | bytes accessed | tf_op | source)
XLA Modules:
  0.0 52.8 jit_solution(15332025517642525676)
XLA Ops:
  0.6 0.0 copy-start.8
  0.6 0.8 %copy.14.taps = f32[32,9]{1,0:T(8,128)S(1)} copy(f32[32,9]{0,1:T(8,128)} %param.12) | data formatting | bytes 2304 | tf_op args[1]
  1.4 0.0 copy-start
  1.4 1.6 %copy-done = bf16[4,32,32,256]{3,2,1,0:T(8,128)(2,1)S(1)} copy-done((bf16[4,32,32,256]{3,2,1,0:T(8,128)(2,1)S(1)}, bf16[4,32,32,256]{3,2,1,0:T(8,128)(2,1)}, u32[]{:S(2)}) %copy-start) | copy-done | bytes 2097176
  3.0 0.0 copy-start.6
  3.0 0.8 %copy-done.6 = f32[32,256]{1,0:T(8,128)S(1)} copy-done((f32[32,256]{1,0:T(8,128)S(1)}, f32[32,256]{1,0:T(8,128)}, u32[]{:S(2)}) %copy-start.6) | copy-done | bytes 32792
  3.8 0.0 copy-start.7
  3.8 0.8 %copy-done.7 = f32[256,32]{0,1:T(8,128)S(1)} copy-done((f32[256,32]{0,1:T(8,128)S(1)}, f32[256,32]{0,1:T(8,128)}, u32[]{:S(2)}) %copy-start.7) | copy-done | bytes 32792
  4.5 0.0 copy-start.9
  4.5 0.7 %copy-done.9 = s32[4]{0:T(128)S(1)} copy-done((s32[4]{0:T(128)S(1)}, s32[4]{0:T(128)}, u32[]{:S(2)}) %copy-start.9) | copy-done | bytes 40
  5.2 0.0 copy-start.1
  5.2 0.0 copy-start.2
  5.2 0.0 copy-start.3
  5.2 0.0 copy-start.4
  5.2 0.0 copy-start.5
  5.2 19.1 %shard_map.130 = (f32[16,256]{1,0:T(8,128)S(1)}, s32[16,128]{1,0:T(8,128)S(1)}, f32[9,32]{1,0:T(8,128)S(1)}) custom-call(s32[4]{0:T(128)S(1)} %copy-done.9, f32[32,9]{1,0:T(8,128)S(1)} %copy.14.taps, bf16[4,32,32,256]{3,2,1,0:T(8,128)(2,1)S(1)} %copy-done, f32[32,256]{1,0:T(8,128)S(1)} %copy-done.6, f32[32,256]{1,0:T(8,128)S(1)} %bitcast.6), custom_call_target="tpu_custom_call" | custom-call | tf_op jit(solution)/shard_map/pallas_call | solution.py:297
  24.4 0.6 %copy.15 = f32[1,32,9]{1,0,2:T(1,128)} copy(f32[1,32,9]{1,2,0:T(8,128)S(1)} %bitcast.7) | data formatting | bytes 2304
  25.0 0.0 copy-done.8
  25.0 0.0 copy-done.1
  25.0 0.0 copy-done.2
  25.0 0.0 copy-done.3
  25.0 0.0 copy-done.4
  25.0 0.0 copy-done.5
  25.0 27.8 %shard_map.131 = (f32[256,256]{1,0:T(8,128)}, f32[4,256]{1,0:T(4,128)}) custom-call(s32[16,128]{1,0:T(8,128)S(1)} %get-tuple-element.8.flags, f32[256,256]{1,0:T(8,128)S(1)} %copy-done.1, f32[256,256]{1,0:T(8,128)S(1)} %copy-done.2, f32[256,256]{1,0:T(8,128)S(1)} %copy-done.3, f32[256,256]{1,0:T(8,128)S(1)} %copy-done.4, f32[256,256]{1,0:T(8,128)S(1)} %copy-done.5, ...), custom_call_target="tpu_custom_call" | custom-call | tf_op jit(solution)/shard_map/pallas_call | solution.py:439
Async XLA Ops:
  0.6 24.3 %copy-start.8 = (f32[256]{0:T(256)S(1)}, f32[256]{0:T(256)}, u32[]{:S(2)}) copy-start(f32[256]{0:T(256)} %param.19) | copy-start | bytes 3076
  1.4 1.6 %copy-start = (bf16[4,32,32,256]{3,2,1,0:T(8,128)(2,1)S(1)}, bf16[4,32,32,256]{3,2,1,0:T(8,128)(2,1)}, u32[]{:S(2)}) copy-start(bf16[4,32,32,256]{3,2,1,0:T(8,128)(2,1)} %x_ref.1) | copy-start | bytes 6291460
  3.0 0.8 %copy-start.6 = (f32[32,256]{1,0:T(8,128)S(1)}, f32[32,256]{1,0:T(8,128)}, u32[]{:S(2)}) copy-start(f32[32,256]{1,0:T(8,128)} %pooling.1) | copy-start | bytes 98308
  3.8 0.8 %copy-start.7 = (f32[256,32]{0,1:T(8,128)S(1)}, f32[256,32]{0,1:T(8,128)}, u32[]{:S(2)}) copy-start(f32[256,32]{0,1:T(8,128)} %param.14) | copy-start | bytes 98308
  4.5 0.7 %copy-start.9 = (s32[4]{0:T(128)S(1)}, s32[4]{0:T(128)}, u32[]{:S(2)}) copy-start(s32[4]{0:T(128)} %flags.1) | copy-start | bytes 52
  5.2 19.8 %copy-start.1 = (f32[256,256]{1,0:T(8,128)S(1)}, f32[256,256]{1,0:T(8,128)}, u32[]{:S(2)}) copy-start(f32[256,256]{1,0:T(8,128)} %quiet_map.1) | copy-start | bytes 786436
  5.2 19.8 %copy-start.2 = (f32[256,256]{1,0:T(8,128)S(1)}, f32[256,256]{1,0:T(8,128)}, u32[]{:S(2)}) copy-start(f32[256,256]{1,0:T(8,128)} %seen_map.1) | copy-start | bytes 786436
  5.2 19.8 %copy-start.3 = (f32[256,256]{1,0:T(8,128)S(1)}, f32[256,256]{1,0:T(8,128)}, u32[]{:S(2)}) copy-start(f32[256,256]{1,0:T(8,128)} %quiet_root.1) | copy-start | bytes 786436
  5.2 19.8 %copy-start.4 = (f32[256,256]{1,0:T(8,128)S(1)}, f32[256,256]{1,0:T(8,128)}, u32[]{:S(2)}) copy-start(f32[256,256]{1,0:T(8,128)} %seen_root.1) | copy-start | bytes 786436
  5.2 19.8 %copy-start.5 = (f32[256,256]{1,0:T(8,128)S(1)}, f32[256,256]{1,0:T(8,128)}, u32[]{:S(2)}) copy-start(f32[256,256]{1,0:T(8,128)} %init_root.1) | copy-start | bytes 786436

commit v3 on v2

--- a/solution.py
+++ b/solution.py
@@ -63,9 +63,10 @@
     return grads
 
 
-def observe_kernel(sizes, flags, taps, x_ref, pooling, gains, shift_ref, flag_ref, grad_ref,
-                   tops, bottoms, lows, highs, pools, sums, grads_all, slots, grad_slots,
-                   halo_send, halo_recv, send_sem, recv_sem, grad_send, grad_recv):
+def observe_kernel(sizes, flags, taps, x_ref, pooling, gains, quiet_map, seen_map, quiet_root, seen_root, init_root,
+                   shift_ref, flag_ref, grad_ref, cov,
+                   tops, bottoms, lows, highs, pools, sums, grads_all, slots, grad_slots, flag_slots, maps, maps_t, grams,
+                   halo_send, halo_recv, send_sem, recv_sem, grad_send, grad_recv, flag_send, flag_recv):
     n_tm, n_space, n_chan = sizes
     steps, channels, rows, width = x_ref.shape
     reach = DILATION_STEP
@@ -100,6 +101,9 @@
             at = pl.ds((g * steps + t) * pack, pack)
             tops[at, :] = jnp.dot(pick_top, x, preferred_element_type=F32).astype(BF16)
             bottoms[at, :] = jnp.dot(pick_bottom, x, preferred_element_type=F32).astype(BF16)
+    prepare_chain(steps, quiet_map, seen_map, quiet_root, seen_root, init_root, maps, maps_t, grams, cov)
+    for t in range(steps):
+        flag_slots[tm, t : t + 1, :] = jnp.zeros((1, 128), F32) + flags[t].astype(F32)
     pl.semaphore_wait(barrier, n_all - 1)
     down = pltpu.make_async_remote_copy(
         src_ref=bottoms, dst_ref=lows, send_sem=halo_send.at[0], recv_sem=halo_recv.at[0],
@@ -116,6 +120,20 @@
     @pl.when(has_last)
     def _():
         up.start()
+
+    def flag_copy(p, slot):
+        return pltpu.make_async_remote_copy(
+            src_ref=flag_slots.at[slot], dst_ref=flag_slots.at[slot], send_sem=flag_send.at[p], recv_sem=flag_recv.at[slot],
+            device_id={"tm": p}, device_id_type=MESH)
+
+    def each(count, mine, act):
+        def turn(i, carry):
+            act(lax.rem(mine + i, count))
+            return carry
+
+        lax.fori_loop(1, count, turn, 0)
+
+    each(n_tm, tm, lambda p: flag_copy(p, tm).start())
 
     pool = pooling[...]
     row_i = lax.broadcasted_iota(jnp.int32, (rows, width), 0)
@@ -139,7 +157,7 @@
         for k in range(9):
             row = jnp.zeros((1, count * each), F32)
             for c in range(count):
-                row = jnp.where(owner == c, taps[first + c, k], row)
+                row = jnp.where(owner == c, taps[k, first + c], row)
             wide.append(row)
         return wide
 
@@ -159,9 +177,9 @@
     def interior(g, carry):
         first = g * group
         for c in range(group):
-            weight = taps[first + c, 0] * pools[0]
+            weight = taps[0, first + c] * pools[0]
             for k in range(1, 9):
-                weight = weight + taps[first + c, k] * pools[k]
+                weight = weight + taps[k, first + c] * pools[k]
             for t in range(steps):
                 part = x_ref[t, first + c].astype(F32) * weight
                 sums[t, pl.ds(first + c, 1), :] = jnp.sum(part, axis=0, keepdims=True)
@@ -233,7 +251,7 @@
             weight = jnp.zeros((edge, width), F32)
             for b in range(3):
                 low_part, high_part = edge_pools[b]
-                weight = weight + taps[first + i, b] * low_part + taps[first + i, 6 + b] * high_part
+                weight = weight + taps[b, first + i] * low_part + taps[6 + b, first + i] * high_part
             for t in range(steps):
                 part = blocks[t][i * edge : (i + 1) * edge, :] * weight
                 at = pl.ds(first + i, 1)
@@ -250,7 +268,6 @@
         tile = jnp.sum(sums[t], axis=1, keepdims=True)
         share = jnp.sum(tile * gains[...], axis=0, keepdims=True) * flag_values[t]
         slots[me, pl.ds(t, 1), :] = share
-        slots[me, pl.ds(steps + t, 1), :] = jnp.zeros((1, share.shape[1]), F32) + flag_values[t]
 
     def share_copy(p, slot):
         return pltpu.make_async_remote_copy(
@@ -262,15 +279,13 @@
             src_ref=grad_slots.at[slot], dst_ref=grad_slots.at[slot], send_sem=grad_send.at[s], recv_sem=grad_recv.at[slot],
             device_id={"space": s}, device_id_type=MESH)
 
-    def each(count, mine, act):
-        def turn(i, carry):
-            act(lax.rem(mine + i, count))
-            return carry
-
-        lax.fori_loop(1, count, turn, 0)
-
     each(n_all, me, lambda p: share_copy(p, me).start())
     each(n_space, space, lambda s: grad_copy(s, space).start())
+    each(n_tm, tm, lambda p: flag_copy(p, p).wait_recv())
+    for block in range(n_tm):
+        for t in range(steps):
+            flag_ref[block * steps + t : block * steps + t + 1, :] = jnp.where(flag_slots[block, t : t + 1, :] > 0.5, 1, 0)
+    run_chain(steps, tm, flag_ref, maps, maps_t, grams, cov)
     each(n_all, me, lambda p: share_copy(p, p).wait_recv())
     each(n_space, space, lambda s: grad_copy(s, s).wait_recv())
     for block in range(n_tm):
@@ -278,46 +293,53 @@
         for part in range(1, n_space * n_chan):
             total = total + slots[block * n_space * n_chan + part, 0:steps, :]
         shift_ref[block * steps : (block + 1) * steps, :] = total
-        marks = slots[block * n_space * n_chan, steps : 2 * steps, 0:128]
-        flag_ref[block * steps : (block + 1) * steps, :] = jnp.where(marks > 0.5, 1, 0)
     total = grad_slots[0]
     for part in range(1, n_space):
         total = total + grad_slots[part]
     grad_ref[...] = total[0:9, 0:channels]
     each(n_all, me, lambda p: share_copy(p, me).wait_send())
     each(n_space, space, lambda s: grad_copy(s, space).wait_send())
-
-
-def observe(flags, taps, frames, pooling, gains):
+    each(n_tm, tm, lambda p: flag_copy(p, tm).wait_send())
+
+
+def observe(flags, taps, frames, pooling, gains, transition, update_map, quiet_root, observed_root, init_root):
     steps, channels, rows, width = frames.shape
     states = gains.shape[1]
     sizes = tuple(lax.axis_size(name) for name in ("tm", "space", "chan"))
     n_all = sizes[0] * sizes[1] * sizes[2]
     packed = steps * channels * DILATION_STEP
+    choices = 4 if steps % 2 == 0 else 2
     return pl.pallas_call(
         functools.partial(observe_kernel, sizes),
-        in_specs=[SMEM, SMEM, VMEM, VMEM, VMEM],
-        out_specs=[VMEM] * 3,
+        in_specs=[SMEM, SMEM] + [VMEM] * 8,
+        out_specs=[VMEM] * 4,
         out_shape=[
             jax.ShapeDtypeStruct((sizes[0] * steps, states), F32),
             jax.ShapeDtypeStruct((sizes[0] * steps, 128), jnp.int32),
             jax.ShapeDtypeStruct((9, channels), F32),
+            jax.ShapeDtypeStruct((states, states), F32),
         ],
         scratch_shapes=[pltpu.VMEM((packed, width), BF16)] * 4 + [
             pltpu.VMEM((9, rows, width), F32),
             pltpu.VMEM((steps, channels, width), F32),
             pltpu.VMEM((16, 128), F32),
-            pltpu.VMEM((n_all, 2 * steps, states), F32),
+            pltpu.VMEM((n_all, 8 * (-(-steps // 8)), states), F32),
             pltpu.VMEM((sizes[1], 16, 128), F32),
+            pltpu.VMEM((sizes[0], 8 * (-(-steps // 8)), 128), F32),
+            pltpu.VMEM((choices, states, 3 * states), BF16),
+            pltpu.VMEM((choices, 3 * states, states), BF16),
+            pltpu.VMEM((choices, states, states), F32),
             pltpu.SemaphoreType.DMA((2,)),
             pltpu.SemaphoreType.DMA((2,)),
             pltpu.SemaphoreType.DMA((n_all,)),
             pltpu.SemaphoreType.DMA((n_all,)),
             pltpu.SemaphoreType.DMA((sizes[1],)),
             pltpu.SemaphoreType.DMA((sizes[1],)),
+            pltpu.SemaphoreType.DMA((sizes[0],)),
+            pltpu.SemaphoreType.DMA((sizes[0],)),
         ],
-        compiler_params=pltpu.CompilerParams(collective_id=0, has_side_effects=True, vmem_limit_bytes=48 * 2**20),
-    )(flags, taps, frames, pooling, gains)
+        compiler_params=pltpu.CompilerParams(collective_id=0, has_side_effects=True, vmem_limit_bytes=60 * 2**20),
+    )(flags, taps, frames, pooling, gains, transition, update_map, quiet_root, observed_root, init_root)
 
 
 def split2(x):
@@ -339,62 +361,98 @@
     return lax.dot_general(lhs, rhs, TN_DIMS, preferred_element_type=F32)
 
 
-def mean_chain(per, tm, flags, quiet_map, seen_map, start, shift_ref, out_ref, maps, maps_t, shifts, columns, lines):
+def left_form(x):
+    h, l = split2(x)
+    return jnp.concatenate([h, h, l], axis=1)
+
+
+def right_form(x):
+    h, l = split2(x)
+    return jnp.concatenate([h, l, h], axis=0)
+
+
+def right_map(x):
+    h, l = split2(x)
+    return jnp.concatenate([h, h, l], axis=0)
+
+
+def left_moving(x):
+    h, l = split2(x)
+    return jnp.concatenate([h, l, h], axis=1)
+
+
+def product(lhs, rhs):
+    return jnp.dot(lhs, rhs, preferred_element_type=F32)
+
+
+def prepare_chain(steps, quiet_map, seen_map, quiet_root, seen_root, init_root, maps, maps_t, grams, cov):
+    cov[...] = gram3(init_root[...])
+    grams[0], grams[1] = gram3(quiet_root[...]), gram3(seen_root[...])
+    single = [(quiet_map[...], grams[0]), (seen_map[...], grams[1])]
+    if steps % 2:
+        joined = single
+    else:
+        joined = []
+        for index, (later, noise) in enumerate(single):
+            lhs = left_form(later)
+            maps_t[index] = right_map(later.T)
+            rhs = maps_t[index]
+            for earlier, earlier_noise in single:
+                moved = product(lhs, right_form(earlier_noise))
+                joined.append((product(lhs, right_form(earlier)), product(left_moving(moved), rhs) + noise))
+    for index, (both, noise) in enumerate(joined):
+        maps[index] = left_form(both)
+        maps_t[index] = right_map(both.T)
+        grams[index] = noise
+
+
+def run_chain(steps, tm, flag_ref, maps, maps_t, grams, cov):
+    paired = steps % 2 == 0
+
+    def advance(t, carry):
+        if paired:
+            which = 2 * flag_ref[2 * t + 1, 0] + flag_ref[2 * t, 0]
+        else:
+            which = flag_ref[t, 0]
+        moved = product(maps[which], right_form(cov[...]))
+        cov[...] = product(left_moving(moved), maps_t[which]) + grams[which]
+        return carry
+
+    lax.fori_loop(0, (tm + 1) * (steps // 2 if paired else steps), advance, 0)
+
+
+def state_kernel(per, flags, cov_ref, quiet_map, seen_map, start_mean, shift_ref, grad_in, out_ref, mean_ref, grad_ref,
+                 cov, panel, held, plain, plain_t, shifts, columns, lines, turned):
+    size = out_ref.shape[0]
     steps = shift_ref.shape[0]
+    tm = lax.axis_index("tm")
+    grad_ref[...] = grad_in[...]
     for index, map_ref in enumerate((quiet_map, seen_map)):
-        maps[index] = map_ref[...]
-        maps_t[index] = map_ref[...].T
+        plain[index] = map_ref[...]
+        plain_t[index] = map_ref[...].T
     shifts[...] = jnp.zeros_like(shifts)
     shifts[0:steps, :] = shift_ref[...]
     columns[...] = shifts[...].T
     lines[...] = jnp.zeros_like(lines)
-    lane = lax.broadcasted_iota(jnp.int32, columns.shape, 1)
-    row = start[...]
-    column = None
-    turned = jnp.zeros(columns.shape, F32)
-    for t in range(steps):
-        flag = flags[t, 0]
-        if t % 2 == 0:
-            column = jnp.sum(maps[flag] * row, axis=1, keepdims=True) + columns[:, t : t + 1]
-            turned = jnp.where(lane == t, column, turned)
-        else:
-            row = jnp.sum(maps_t[flag] * column, axis=0, keepdims=True) + shifts[t : t + 1, :]
-            lines[t : t + 1, :] = row
-    lines[...] = lines[...] + turned.T
-    for block in range(steps // per):
-
-        @pl.when(tm == block)
-        def _():
-            out_ref[...] = lines[block * per : (block + 1) * per, :]
-
-
-def state_kernel(per, flags, quiet_map, seen_map, quiet_root, seen_root, init_root, start_mean, shift_ref, out_ref, mean_ref, maps, maps_t, grams, cov, panel, held, plain, plain_t, shifts, columns, lines):
-    size = out_ref.shape[0]
-    tm = lax.axis_index("tm")
-    mean_chain(per, tm, flags, quiet_map, seen_map, start_mean, shift_ref, mean_ref, plain, plain_t, shifts, columns, lines)
-    for index, (map_ref, root_ref) in enumerate(((quiet_map, quiet_root), (seen_map, seen_root))):
-        h, l = split2(map_ref[...])
-        maps[index] = jnp.concatenate([h, h, l], axis=1)
-        h, l = split2(map_ref[...].T)
-        maps_t[index] = jnp.concatenate([h, h, l], axis=0)
-        grams[index] = gram3(root_ref[...])
-    cov[...] = gram3(init_root[...])
-
-    def advance(t, carry):
-        flag = flags[t, 0]
-        h, l = split2(cov[...])
-        moved = jnp.dot(maps[flag], jnp.concatenate([h, l, h], axis=0), preferred_element_type=F32)
-        h, l = split2(moved)
-        cov[...] = jnp.dot(jnp.concatenate([h, l, h], axis=1), maps_t[flag], preferred_element_type=F32) + grams[flag]
-        return carry
-
-    lax.fori_loop(0, (tm + 1) * per, advance, 0)
-
+    turned[...] = jnp.zeros_like(turned)
+    lane_t = lax.broadcasted_iota(jnp.int32, columns.shape, 1)
     lane = lax.broadcasted_iota(jnp.int32, (8, size), 1)
     held[...] = jnp.zeros_like(held)
-    panel[...] = cov[0:NB, :]
-
-    def block(b, carry):
+    cov[...] = cov_ref[...]
+    panel[...] = cov_ref[0:NB, :]
+
+    def column_step(t, row):
+        shift = jnp.sum(jnp.where(lane_t == t, columns[...], 0.0), axis=1, keepdims=True)
+        column = jnp.sum(plain[flags[t, 0]] * row, axis=1, keepdims=True) + shift
+        turned[...] = jnp.where(lane_t == t, column, turned[...])
+        return column
+
+    def row_step(t, column):
+        row = jnp.sum(plain_t[flags[t, 0]] * column, axis=0, keepdims=True) + shifts[pl.ds(t, 1), :]
+        lines[pl.ds(t, 1), :] = row
+        return row
+
+    def block(b):
         start = pl.multiple_of(b * NB, NB)
         before = held[...]
         rows = panel[...]
@@ -404,47 +462,67 @@
         for k in range(NB):
             for i in range(k + 1):
                 d[i][k] = jnp.broadcast_to(wide[k][i : i + 1, :], (8, 128))
-        lines = [jnp.broadcast_to(panel[i : i + 1, :], (8, size)) for i in range(NB)]
+        lines_b = [jnp.broadcast_to(panel[i : i + 1, :], (8, size)) for i in range(NB)]
+        spread = lambda v: jnp.concatenate([v] * (size // 128), axis=1)
         for j in range(NB):
-            r = lax.rsqrt(d[j][j])
-            r = r * (1.5 - 0.5 * d[j][j] * r * r)
-            u = {k: d[j][k] * r for k in range(j + 1, NB)}
-            twice = jnp.concatenate([r] * (size // 128), axis=1)
-            line = jnp.where(lane >= start + j, lines[j] * twice, 0.0)
-            held[j : j + 1, :] = line[0:1, :]
+            pivot = d[j][j]
+            r = lax.rsqrt(pivot)
+            r = r * (1.5 - 0.5 * pivot * r * r)
+            held[j : j + 1, :] = jnp.where(lane >= start + j, lines_b[j] * spread(r), 0.0)[0:1, :]
+            if j == NB - 1:
+                break
+            inverse = 1.0 / pivot
             for i in range(j + 1, NB):
-                lines[i] = lines[i] - jnp.concatenate([u[i]] * (size // 128), axis=1) * line
+                ratio = d[j][i] * inverse
                 for k in range(i, NB):
-                    d[i][k] = d[i][k] - u[i] * u[k]
+                    d[i][k] = d[i][k] - ratio * d[j][k]
+                lines_b[i] = lines_b[i] - spread(ratio) * lines_b[j]
         cov[...] = cov[...] - gram3(before)
         done = held[...]
         out_ref[pl.ds(start, NB), :] = done
         after = lax.rem(start + NB, size)
-        turned = pltpu.roll(done, lax.rem(size - after, size), 1)[:, 0:128]
+        following = pltpu.roll(done, lax.rem(size - after, size), 1)[:, 0:128]
         h, m, l = split3(done)
-        p, q, s = split3(turned)
+        p, q, s = split3(following)
         lhs = jnp.concatenate([p, p, q, p, s, q], axis=0)
         rhs = jnp.concatenate([h, m, h, l, h, m], axis=0)
         change = lax.dot_general(lhs, rhs, TN_DIMS, preferred_element_type=F32)
         panel[...] = cov[pl.ds(pl.multiple_of(after, NB), NB), :] - change[0:NB, :]
-        return carry
-
-    lax.fori_loop(0, size // NB, block, 0)
-
-
-def state(per, flags, transition, update_map, quiet_root, observed_root, init_root, init_mean, shifts):
+
+    pairs = size // (2 * NB)
+    turns = -(-steps // (2 * pairs))
+
+    def two_blocks(v, row):
+        for i in range(turns):
+            t = 2 * (v * turns + i)
+            row = row_step(t + 1, column_step(t, row))
+        block(2 * v)
+        block(2 * v + 1)
+        return row
+
+    lax.fori_loop(0, pairs, two_blocks, start_mean[...])
+    lines[...] = lines[...] + turned[...].T
+    for i in range(steps // per):
+
+        @pl.when(tm == i)
+        def _():
+            mean_ref[...] = lines[i * per : (i + 1) * per, :]
+
+
+def state(per, flags, cov, transition, update_map, init_mean, shifts, grads):
     size = transition.shape[0]
     steps = shifts.shape[0]
     padded = -(-steps // 128) * 128
     return pl.pallas_call(
         functools.partial(state_kernel, per),
-        in_specs=[SMEM] + [VMEM] * 7,
-        out_specs=[VMEM] * 2,
-        out_shape=[jax.ShapeDtypeStruct((size, size), F32), jax.ShapeDtypeStruct((per, size), F32)],
+        in_specs=[SMEM] + [VMEM] * 6,
+        out_specs=[VMEM] * 3,
+        out_shape=[
+            jax.ShapeDtypeStruct((size, size), F32),
+            jax.ShapeDtypeStruct((per, size), F32),
+            jax.ShapeDtypeStruct(grads.shape, F32),
+        ],
         scratch_shapes=[
-            pltpu.VMEM((2, size, 3 * size), BF16),
-            pltpu.VMEM((2, 3 * size, size), BF16),
-            pltpu.VMEM((2, size, size), F32),
             pltpu.VMEM((size, size), F32),
             pltpu.VMEM((NB, size), F32),
             pltpu.VMEM((NB, size), F32),
@@ -453,16 +531,18 @@
             pltpu.VMEM((padded, size), F32),
             pltpu.VMEM((size, padded), F32),
             pltpu.VMEM((padded, size), F32),
+            pltpu.VMEM((size, padded), F32),
         ],
-        compiler_params=pltpu.CompilerParams(vmem_limit_bytes=48 * 2**20),
-    )(flags, transition, update_map, quiet_root, observed_root, init_root, init_mean[None], shifts)
+        compiler_params=pltpu.CompilerParams(vmem_limit_bytes=60 * 2**20),
+    )(flags, cov, transition, update_map, init_mean[None], shifts, grads)
 
 
 def local(frames, conv_taps, pooling, gain_matrix, transition, update_map, quiet_root, observed_root, init_mean, init_root, observed):
-    per = frames.shape[0]
-    shifts, flags, tap_gradient = observe(observed, conv_taps, frames, pooling, gain_matrix.T)
-    roots, filtered_means = state(per, flags, transition, update_map, quiet_root, observed_root, init_root, init_mean, shifts)
-    return (filtered_means, roots[None], tap_gradient.T[None])
+    shifts, flags, grads, cov = observe(
+        observed, conv_taps.T, frames, pooling, gain_matrix.T, transition, update_map, quiet_root, observed_root, init_root
+    )
+    roots, filtered_means, grads = state(frames.shape[0], flags, cov, transition, update_map, init_mean, shifts, grads)
+    return (filtered_means, roots[None], grads.T[None])
 
 
 def solution(mesh):

time: 53.1 us -> 41.1 us (0.77)
  the two profiles are of different devices: /device:TPU:27 before, /device:TPU:0 now
where the time goes in v3:
time: 41.1 us; the launch traced here: 40.9 us
  Pallas kernels  38.9 us (95%)
  local copies, waits for them, and re-layouts  1.29 us (3%)
  between operations  0.64 us (2%)
    pallas_call x1, Pallas kernels, observe(): pl.pallas_call(functools.partial(observe_kernel, sizes), in_specs=[SMEM,...  23.9 us
    pallas_call x1, Pallas kernels, state(): pl.pallas_call(functools.partial(state_kernel, per), in_specs=[SMEM] + [V...  15 us
    unnamed x1, local copies, waits for them, and re-layouts  1.29 us

profile of v3, /device:TPU:0, one launch (start us, length us, event | category | flops | bytes accessed | tf_op | source)
XLA Modules:
  0.0 40.9 jit_solution(16072848976543441057)
XLA Ops:
  0.6 23.9 %shard_map.130 = (f32[16,256]{1,0:T(8,128)}, s32[16,128]{1,0:T(8,128)}, f32[9,32]{1,0:T(8,128)}, f32[256,256]{1,0:T(8,128)}) custom-call(s32[4]{0:T(128)} %flags.1, f32[9,32]{1,0:T(8,128)} %bitcast.8, bf16[4,32,32,256]{3,2,1,0:T(8,128)(2,1)} %x_ref.1, f32[32,256]{1,0:T(8,128)} %pooling.1, f32[32,256]{1,0:T(8,128)} %bitcast.7, f32[256,256]{1,0:T(8,128)} %quiet_map.3, ...), custom_call_target="tpu_custom_call" | custom-call | tf_op jit(solution)/shard_map/pallas_call | solution.py:312
  24.6 15.0 %shard_map.131 = (f32[256,256]{1,0:T(8,128)}, f32[4,256]{1,0:T(4,128)}, f32[9,32]{1,0:T(8,128)}) custom-call(s32[16,128]{1,0:T(8,128)} %get-tuple-element.10.flags, f32[256,256]{1,0:T(8,128)} %get-tuple-element.11.cov_ref, f32[256,256]{1,0:T(8,128)} %quiet_map.3, f32[256,256]{1,0:T(8,128)} %seen_map.3, f32[1,256]{1,0:T(1,128)} %bitcast.10, ...), custom_call_target="tpu_custom_call" | custom-call | tf_op jit(solution)/shard_map/pallas_call | solution.py:516
  39.6 1.3 %copy.14 = f32[1,32,9]{1,0,2:T(1,128)} copy(f32[1,32,9]{1,2,0:T(8,128)} %bitcast.9) | data formatting | bytes 2304

commit v4 on v3

--- a/solution.py
+++ b/solution.py
@@ -426,7 +426,8 @@
     size = out_ref.shape[0]
     steps = shift_ref.shape[0]
     tm = lax.axis_index("tm")
-    grad_ref[...] = grad_in[...]
+    for k in range(grad_in.shape[0]):
+        grad_ref[k] = grad_in[k : k + 1, :]
     for index, map_ref in enumerate((quiet_map, seen_map)):
         plain[index] = map_ref[...]
         plain_t[index] = map_ref[...].T
@@ -436,7 +437,8 @@
     lines[...] = jnp.zeros_like(lines)
     turned[...] = jnp.zeros_like(turned)
     lane_t = lax.broadcasted_iota(jnp.int32, columns.shape, 1)
-    lane = lax.broadcasted_iota(jnp.int32, (8, size), 1)
+    lane = lax.broadcasted_iota(jnp.int32, (NB, size), 1)
+    line = lax.broadcasted_iota(jnp.int32, (NB, size), 0)
     held[...] = jnp.zeros_like(held)
     cov[...] = cov_ref[...]
     panel[...] = cov_ref[0:NB, :]
@@ -458,25 +460,23 @@
         rows = panel[...]
         corner = pltpu.roll(rows, lax.rem(size - start, size), 1)[:, 0:128]
         wide = [jnp.broadcast_to(corner[:, k : k + 1], (NB, 128)) for k in range(NB)]
-        d = [[None] * NB for _ in range(NB)]
-        for k in range(NB):
-            for i in range(k + 1):
-                d[i][k] = jnp.broadcast_to(wide[k][i : i + 1, :], (8, 128))
-        lines_b = [jnp.broadcast_to(panel[i : i + 1, :], (8, size)) for i in range(NB)]
+        row_n = lax.broadcasted_iota(jnp.int32, (NB, 128), 0)
         spread = lambda v: jnp.concatenate([v] * (size // 128), axis=1)
+        scales = jnp.zeros((NB, 128), F32)
         for j in range(NB):
-            pivot = d[j][j]
-            r = lax.rsqrt(pivot)
-            r = r * (1.5 - 0.5 * pivot * r * r)
-            held[j : j + 1, :] = jnp.where(lane >= start + j, lines_b[j] * spread(r), 0.0)[0:1, :]
+            pivot = jnp.broadcast_to(wide[j][j : j + 1, :], (NB, 128))
+            scales = jnp.where(row_n == j, pivot, scales)
             if j == NB - 1:
                 break
-            inverse = 1.0 / pivot
-            for i in range(j + 1, NB):
-                ratio = d[j][i] * inverse
-                for k in range(i, NB):
-                    d[i][k] = d[i][k] - ratio * d[j][k]
-                lines_b[i] = lines_b[i] - spread(ratio) * lines_b[j]
+            inverse = pl.reciprocal(pivot, approx=True)
+            inverse = inverse * (2.0 - pivot * inverse)
+            ratio = jnp.where(row_n > j, wide[j] * inverse, 0.0)
+            for k in range(j + 1, NB):
+                wide[k] = wide[k] - ratio * jnp.broadcast_to(wide[k][j : j + 1, :], (NB, 128))
+            rows = rows - spread(ratio) * jnp.broadcast_to(rows[j : j + 1, :], (NB, size))
+        r = lax.rsqrt(scales)
+        r = r * (1.5 - 0.5 * scales * r * r)
+        held[...] = jnp.where(lane >= start + line, rows * spread(r), 0.0)
         cov[...] = cov[...] - gram3(before)
         done = held[...]
         out_ref[pl.ds(start, NB), :] = done
@@ -520,7 +520,7 @@
         out_shape=[
             jax.ShapeDtypeStruct((size, size), F32),
             jax.ShapeDtypeStruct((per, size), F32),
-            jax.ShapeDtypeStruct(grads.shape, F32),
+            jax.ShapeDtypeStruct((grads.shape[0], 1, grads.shape[1]), F32),
         ],
         scratch_shapes=[
             pltpu.VMEM((size, size), F32),
@@ -542,7 +542,7 @@
         observed, conv_taps.T, frames, pooling, gain_matrix.T, transition, update_map, quiet_root, observed_root, init_root
     )
     roots, filtered_means, grads = state(frames.shape[0], flags, cov, transition, update_map, init_mean, shifts, grads)
-    return (filtered_means, roots[None], grads.T[None])
+    return (filtered_means, roots[None], jnp.transpose(grads, (1, 2, 0)))
 
 
 def solution(mesh):

time: 41.1 us -> 37.6 us (0.915)
  Pallas kernels: 38.9 us -> 36.8 us
  local copies, waits for them, and re-layouts: 1.29 us -> 0 us
    pallas_call x1, Pallas kernels: 15 us -> 12.8 us  [state(): pl.pallas_call(functools.partial(state_kernel, per), in_specs=[SMEM] + [V...]
    unnamed x1 -> x0, local copies, waits for them, and re-layouts: 1.29 us -> none
where the time goes in v4:
time: 37.6 us; the launch traced here: 37.4 us
  Pallas kernels  36.8 us (98%)
  between operations  0.64 us (2%)
    pallas_call x1, Pallas kernels, observe(): pl.pallas_call(functools.partial(observe_kernel, sizes), in_specs=[SMEM,...  23.9 us
    pallas_call x1, Pallas kernels, state(): pl.pallas_call(functools.partial(state_kernel, per), in_specs=[SMEM] + [V...  12.8 us

profile of v4, /device:TPU:0, one launch (start us, length us, event | category | flops | bytes accessed | tf_op | source)
XLA Modules:
  0.0 37.4 jit_solution(18280217653545839205)
XLA Ops:
  0.6 23.9 %shard_map.130 = (f32[16,256]{1,0:T(8,128)}, s32[16,128]{1,0:T(8,128)}, f32[9,32]{1,0:T(8,128)}, f32[256,256]{1,0:T(8,128)}) custom-call(s32[4]{0:T(128)} %flags.1, f32[9,32]{1,0:T(8,128)} %bitcast.6, bf16[4,32,32,256]{3,2,1,0:T(8,128)(2,1)} %x_ref.1, f32[32,256]{1,0:T(8,128)} %pooling.1, f32[32,256]{1,0:T(8,128)} %bitcast.5, f32[256,256]{1,0:T(8,128)} %quiet_map.3, ...), custom_call_target="tpu_custom_call" | custom-call | tf_op jit(solution)/shard_map/pallas_call | solution.py:312
  24.6 12.8 %shard_map.131 = (f32[256,256]{1,0:T(8,128)}, f32[4,256]{1,0:T(4,128)}, f32[9,1,32]{2,1,0:T(1,128)}) custom-call(s32[16,128]{1,0:T(8,128)} %get-tuple-element.10.flags, f32[256,256]{1,0:T(8,128)} %get-tuple-element.11.cov_ref, f32[256,256]{1,0:T(8,128)} %quiet_map.3, f32[256,256]{1,0:T(8,128)} %seen_map.3, f32[1,256]{1,0:T(1,128)} %bitcast.7, ...), custom_call_target="tpu_custom_call" | custom-call | tf_op jit(solution)/shard_map/pallas_call | solution.py:516

commit v5 on v4

--- a/solution.py
+++ b/solution.py
@@ -101,40 +101,6 @@
             at = pl.ds((g * steps + t) * pack, pack)
             tops[at, :] = jnp.dot(pick_top, x, preferred_element_type=F32).astype(BF16)
             bottoms[at, :] = jnp.dot(pick_bottom, x, preferred_element_type=F32).astype(BF16)
-    prepare_chain(steps, quiet_map, seen_map, quiet_root, seen_root, init_root, maps, maps_t, grams, cov)
-    for t in range(steps):
-        flag_slots[tm, t : t + 1, :] = jnp.zeros((1, 128), F32) + flags[t].astype(F32)
-    pl.semaphore_wait(barrier, n_all - 1)
-    down = pltpu.make_async_remote_copy(
-        src_ref=bottoms, dst_ref=lows, send_sem=halo_send.at[0], recv_sem=halo_recv.at[0],
-        device_id={"space": lax.rem(space + 1, n_space)}, device_id_type=MESH)
-    up = pltpu.make_async_remote_copy(
-        src_ref=tops, dst_ref=highs, send_sem=halo_send.at[1], recv_sem=halo_recv.at[1],
-        device_id={"space": lax.rem(space + n_space - 1, n_space)}, device_id_type=MESH)
-    has_next, has_last = space < n_space - 1, space > 0
-
-    @pl.when(has_next)
-    def _():
-        down.start()
-
-    @pl.when(has_last)
-    def _():
-        up.start()
-
-    def flag_copy(p, slot):
-        return pltpu.make_async_remote_copy(
-            src_ref=flag_slots.at[slot], dst_ref=flag_slots.at[slot], send_sem=flag_send.at[p], recv_sem=flag_recv.at[slot],
-            device_id={"tm": p}, device_id_type=MESH)
-
-    def each(count, mine, act):
-        def turn(i, carry):
-            act(lax.rem(mine + i, count))
-            return carry
-
-        lax.fori_loop(1, count, turn, 0)
-
-    each(n_tm, tm, lambda p: flag_copy(p, tm).start())
-
     pool = pooling[...]
     row_i = lax.broadcasted_iota(jnp.int32, (rows, width), 0)
     lane_i = lax.broadcasted_iota(jnp.int32, (rows, width), 1)
@@ -189,6 +155,40 @@
         return carry
 
     lax.fori_loop(0, groups, interior, 0)
+
+    for t in range(steps):
+        flag_slots[tm, t : t + 1, :] = jnp.zeros((1, 128), F32) + flags[t].astype(F32)
+    pl.semaphore_wait(barrier, n_all - 1)
+    down = pltpu.make_async_remote_copy(
+        src_ref=bottoms, dst_ref=lows, send_sem=halo_send.at[0], recv_sem=halo_recv.at[0],
+        device_id={"space": lax.rem(space + 1, n_space)}, device_id_type=MESH)
+    up = pltpu.make_async_remote_copy(
+        src_ref=tops, dst_ref=highs, send_sem=halo_send.at[1], recv_sem=halo_recv.at[1],
+        device_id={"space": lax.rem(space + n_space - 1, n_space)}, device_id_type=MESH)
+    has_next, has_last = space < n_space - 1, space > 0
+
+    @pl.when(has_next)
+    def _():
+        down.start()
+
+    @pl.when(has_last)
+    def _():
+        up.start()
+
+    def flag_copy(p, slot):
+        return pltpu.make_async_remote_copy(
+            src_ref=flag_slots.at[slot], dst_ref=flag_slots.at[slot], send_sem=flag_send.at[p], recv_sem=flag_recv.at[slot],
+            device_id={"tm": p}, device_id_type=MESH)
+
+    def each(count, mine, act):
+        def turn(i, carry):
+            act(lax.rem(mine + i, count))
+            return carry
+
+        lax.fori_loop(1, count, turn, 0)
+
+    each(n_tm, tm, lambda p: flag_copy(p, tm).start())
+    prepare_chain(steps, quiet_map, seen_map, quiet_root, seen_root, init_root, maps, maps_t, grams, cov)
 
     @pl.when(has_last)
     def _():

time: 37.6 us -> 39.3 us (1.045)
  Pallas kernels: 36.8 us -> 38.5 us
    pallas_call x1, Pallas kernels: 23.9 us -> 25.7 us  [observe(): pl.pallas_call(functools.partial(observe_kernel, sizes), in_specs=[SMEM,...]
where the time goes in v5:
time: 39.3 us; the launch traced here: 39.2 us
  Pallas kernels  38.5 us (98%)
  between operations  0.64 us (2%)
    pallas_call x1, Pallas kernels, observe(): pl.pallas_call(functools.partial(observe_kernel, sizes), in_specs=[SMEM,...  25.7 us
    pallas_call x1, Pallas kernels, state(): pl.pallas_call(functools.partial(state_kernel, per), in_specs=[SMEM] + [V...  12.8 us

profile of v5, /device:TPU:0, one launch (start us, length us, event | category | flops | bytes accessed | tf_op | source)
XLA Modules:
  0.0 39.2 jit_solution(5423626044555310536)
XLA Ops:
  0.6 25.7 %shard_map.130 = (f32[16,256]{1,0:T(8,128)}, s32[16,128]{1,0:T(8,128)}, f32[9,32]{1,0:T(8,128)}, f32[256,256]{1,0:T(8,128)}) custom-call(s32[4]{0:T(128)} %flags.1, f32[9,32]{1,0:T(8,128)} %bitcast.6, bf16[4,32,32,256]{3,2,1,0:T(8,128)(2,1)} %x_ref.1, f32[32,256]{1,0:T(8,128)} %pooling.1, f32[32,256]{1,0:T(8,128)} %bitcast.5, f32[256,256]{1,0:T(8,128)} %quiet_map.3, ...), custom_call_target="tpu_custom_call" | custom-call | tf_op jit(solution)/shard_map/pallas_call | solution.py:312
  26.3 12.8 %shard_map.131 = (f32[256,256]{1,0:T(8,128)}, f32[4,256]{1,0:T(4,128)}, f32[9,1,32]{2,1,0:T(1,128)}) custom-call(s32[16,128]{1,0:T(8,128)} %get-tuple-element.10.flags, f32[256,256]{1,0:T(8,128)} %get-tuple-element.11.cov_ref, f32[256,256]{1,0:T(8,128)} %quiet_map.3, f32[256,256]{1,0:T(8,128)} %seen_map.3, f32[1,256]{1,0:T(1,128)} %bitcast.7, ...), custom_call_target="tpu_custom_call" | custom-call | tf_op jit(solution)/shard_map/pallas_call | solution.py:516
